TPU v7x, 256 devices: a whole 4x4x8 slice. The times are simulated.
256 devices in a mesh: grp: 8 (over y, core), col: 32 (over x, z).
Axes of the slice: x: 4, y: 4, z: 8, core: 2. Of those that a mesh axis runs over, the one named last changes fastest.
Arguments:
- tiles: float32 [8, 32, 192, 128, 128], P('grp', 'col')
- tile_rows: int32 [8, 32, 192], P('grp', 'col'), may hold values from 0 to 31
- tile_cols: int32 [8, 32, 192], P('grp', 'col'), may hold values from 0 to 3
- bucket_fill: int32 [8, 32, 32], P('grp', 'col'), may hold values from 1 to 6, as said below
- row_slot: int32 [8, 32], P('grp'), may hold values from 0 to 31, each once within a row
- sketch: float32 [16384, 256], P('col'), may hold values from -6 to 6
Outputs:
- embedding: float32 [32768, 256], P(('grp', 'col'))
- factor: float32 [256, 256], replicated
Inputs may be any that keep to these rules, and one draw needn't show every extreme that they name: `bucket_fill`: every device has at least one bucket with all 6 slots live.
All inputs are finite; a program needn't handle non-finite values.
Results may differ from a plain program's by a relative error of at most 0.0003.
Values sent between devices are 32-bit elements; how exact they have to be, the bound alone decides.
No kernel may reach another device: no remote copies, remote signals or barrier semaphores. Data moves between devices by JAX's collectives and lax.ppermute only.
A program may use at most 192 MiB of HBM per device.

v0:
```python
import jax
import jax.numpy as jnp
from jax import lax
from jax.sharding import PartitionSpec as P


def on_device(tiles, tile_rows, tile_cols, bucket_fill, row_slot, sketch):
    shard_count = lax.axis_size("col")
    tile_stack = tiles[0, 0]
    slot_total = tile_stack.shape[0]
    per_bucket = slot_total // shard_count
    tile_edge = tile_stack.shape[1]
    sketch_width = sketch.shape[1]
    blocks_dev = sketch.shape[0] // tile_edge
    rows_here = tile_rows[0, 0]
    cols_here = tile_cols[0, 0]
    fill_counts = bucket_fill[0, 0]
    slot_table = row_slot[0]
    group_blocks = slot_table.shape[0]
    block_ids = jnp.arange(group_blocks, dtype=jnp.int32)
    target = jnp.sum(
        jnp.where(rows_here[:, None] == block_ids[None, :], slot_table[None, :], 0), axis=1
    )
    slot_ids = jnp.arange(slot_total, dtype=jnp.int32)
    bucket_of = slot_ids // per_bucket
    bucket_ids = jnp.arange(shard_count, dtype=jnp.int32)
    fill_of = jnp.sum(
        jnp.where(bucket_of[:, None] == bucket_ids[None, :], fill_counts[None, :], 0), axis=1
    )
    live_flag = (slot_ids % per_bucket < fill_of).astype(jnp.int32)
    piece = lax.all_gather(sketch, "col", axis=0, tiled=True)
    piece_buckets = piece.shape[0] // (blocks_dev * tile_edge)
    slot_count = piece_buckets * per_bucket
    local_index = jnp.arange(slot_count, dtype=jnp.int32) // per_bucket * blocks_dev + cols_here
    panel_blocks = piece.reshape(piece_buckets * blocks_dev, tile_edge, sketch_width)
    panels = jnp.take(panel_blocks, local_index, axis=0)
    products = jnp.einsum("tij,tjk->tik", tile_stack, panels, precision=lax.Precision.HIGHEST)
    selector = ((target[None, :] == block_ids[:, None]) & (live_flag[None, :] > 0)).astype(
        jnp.float32
    )
    partial_slab = jnp.einsum("st,tik->sik", selector, products, precision=lax.Precision.HIGHEST)
    owned_rows = lax.psum_scatter(partial_slab, "col", scatter_dimension=0, tiled=True)
    product_rows = owned_rows.reshape(-1, sketch_width)
    gram_local = jnp.dot(
        product_rows.T,
        product_rows,
        precision=lax.Precision.HIGHEST,
        preferred_element_type=jnp.float32,
    )
    gram_matrix = lax.psum(gram_local, ("grp", "col"))
    lower_factor = jnp.linalg.cholesky(gram_matrix)
    total_rows = product_rows.shape[0] * lax.axis_size("grp") * shard_count
    row_scale = jnp.sqrt(jnp.float32(total_rows))
    solved = lax.linalg.triangular_solve(
        lower_factor, product_rows, left_side=False, lower=True, transpose_a=True
    )
    embedding = solved * row_scale
    factor = lower_factor.T / row_scale
    return (embedding, factor)


def solution(mesh):
    placed = (
        P("grp", "col", None, None, None),
        P("grp", "col", None),
        P("grp", "col", None),
        P("grp", "col", None),
        P("grp", None),
        P("col", None),
    )
    return jax.shard_map(
        on_device,
        mesh=mesh,
        in_specs=placed,
        out_specs=(P(("grp", "col"), None), P()),
        check_vma=False,
    )
```

profile of v0, /device:TPU:1, one launch (start us, length us, event | category | flops | bytes accessed | tf_op | source)
XLA Modules:
  0.0 811.3 jit_solution(5898187212754187940)
XLA Ops:
  7.2 0.0 all-gather.2.cloned.1.call-start
  7.2 0.7 all-gather.2.cloned.1.call-update
  7.9 0.0 reduce-scatter.2.cloned.1.call-start
  8.0 0.7 compare_select_fusion
  8.7 0.7 select_reduce_fusion.2
  9.4 0.8 select_reduce_fusion.3
  10.2 0.7 compare_and_fusion
  10.9 143.6 %all-gather.2.cloned.1.call-done = f32[16384,256]{1,0:T(8,128)} async-done(((f32[512,256]{1,0:T(8,128)}), f32[16384,256]{1,0:T(8,128)}) %all-gather.2.cloned.1.call-update) | async-done | bytes 16777232 | tf_op jit(solution)/shard_map/all_gather | solution.py:31
  154.6 18.2 %gather_fusion = f32[192,128,256]{2,1,0:T(8,128)} fusion(f32[128,128,256]{2,1,0:T(8,128)} %bitcast.55, s32[1024]{0:T(1024)S(1)} %pad_clamp_fusion), kind=kCustom, calls=%fused_computation | custom fusion | bytes 50332416 | tf_op jit(solution)/shard_map/jit(_take)/gather | solution.py:36
  172.7 49.4 %fusion.5 = f32[192,128,256]{1,2,0:T(8,128)} fusion(f32[1,1,192,128,128]{4,3,2,1,0:T(8,128)} %param.6, f32[192,128,256]{2,1,0:T(8,128)} %gather_fusion, pred[192]{0:T(512)(128)(4,1)S(1)} %compare_and_fusion), kind=kOutput, calls=%fused_computation.8 | convolution fusion | flops 9669967872 | bytes 62914752 | tf_op jit(solution)/shard_map/tij,tjk->tik/dot_general | solution.py:37
  222.1 24.8 %copy.30 = f32[192,128,256]{2,0,1:T(8,128)} copy(f32[192,128,256]{1,2,0:T(8,128)} %fusion.5) | data formatting | bytes 50331648 | tf_op jit(solution)/shard_map/tij,tjk->tik/dot_general | solution.py:37
  246.9 14.6 %fusion.21 = f32[32,128,256]{2,0,1:T(8,128)S(1)} fusion(f32[192,128,256]{2,0,1:T(8,128)} %copy.30, s32[192]{0:T(256)S(1)} %select_reduce_fusion.3, pred[192]{0:T(512)(128)(4,1)S(1)} %fusion.28), kind=kOutput, calls=%fused_computation.39 | convolution fusion | flops 2415931392 | bytes 29361088 | tf_op jit(solution)/shard_map/st,tik->sik/dot_general | solution.py:41
  261.5 4.4 copy.31
  265.8 0.0 reduce-scatter.2.cloned.1.call-update
  265.9 0.3 all-reduce.3.cloned.1.call-start
  266.1 213.1 %reduce-scatter.2.cloned.1.call-done = f32[1,128,256]{2,1,0:T(8,128)} async-done(((f32[32,128,256]{2,1,0:T(8,128)}), f32[1,128,256]{2,1,0:T(8,128)}) %reduce-scatter.2.cloned.1.call-update) | async-done | bytes 131088 | tf_op jit(solution)/shard_map/reduce_scatter | solution.py:42
  479.2 2.1 fusion.29
  481.3 0.0 all-reduce.3.cloned.1.call-update
  481.4 257.1 %all-reduce.3.cloned.1.call-done = f32[256,256]{0,1:T(8,128)} async-done(((f32[256,256]{0,1:T(8,128)}), f32[256,256]{0,1:T(8,128)}) %all-reduce.3.cloned.1.call-update) | async-done | bytes 262160 | tf_op jit(solution)/shard_map/psum | solution.py:50
  738.4 1.1 copy.33
  739.5 1.0 fusion.10
  740.5 11.7 %cholesky.50 = f32[128,128]{1,0:T(8,128)S(1)} custom-call(f32[128,128]{1,0:T(8,128)S(1)} %cholesky.118), custom_call_target="Cholesky" | custom-call | tf_op jit(solution)/shard_map/jit(cholesky)/cholesky | solution.py:51
  752.3 9.8 %custom-call.14 = f32[1,128,128]{1,2,0:T(8,128)S(1)} custom-call(f32[1,128,128]{2,1,0:T(8,128)S(1)} %get-tuple-element.35), custom_call_target="InvertDiagBlocksLowerTriangular" | custom-call | tf_op jit(solution)/shard_map/jit(cholesky)/cholesky | solution.py:51
  762.1 0.2 constant_dynamic-update-slice_fusion.1
  762.3 0.3 convolution_subtract_fusion.1
  762.6 11.7 %cholesky.105 = f32[128,128]{1,0:T(8,128)S(1)} custom-call(f32[128,128]{1,0:T(8,128)S(1)} %convolution_subtract_fusion.1), custom_call_target="Cholesky" | custom-call | tf_op jit(solution)/shard_map/jit(cholesky)/cholesky | solution.py:51
  774.4 0.7 compare_reduce_fusion
  776.5 0.1 triangular_solve.58
  776.5 4.3 while.1
  776.8 0.6 fusion.39
  777.4 1.4 bitcast_dynamic-update-slice_fusion.2
  778.8 0.6 fusion.39
  779.4 1.4 bitcast_dynamic-update-slice_fusion.2
  780.9 19.7 %custom-call.15 = f32[2,128,128]{1,2,0:T(8,128)S(1)} custom-call(f32[2,128,128]{2,1,0:T(8,128)S(1)} %get-tuple-element.9), custom_call_target="InvertDiagBlocksLowerTriangular" | custom-call | tf_op jit(solution)/shard_map/triangular_solve | solution.py:54
  800.5 1.1 fusion.14
  801.7 1.1 convolution_subtract_fusion
  802.8 0.3 fusion.12
  803.1 0.8 copy.34
  803.9 0.8 copy.35
  (13 shorter events, 0.2 us)
Async XLA Ops:
  7.2 147.4 %all-gather.2.cloned.1.call-start = ((), (), s32[]{:S(2)}) async-start(), calls=%async_computation.1 | async-start | bytes 17301504 | tf_op jit(solution)/shard_map/all_gather | solution.py:31
  7.9 471.3 %reduce-scatter.2.cloned.1.call-start = ((), (), s32[]{:S(2)}) async-start(), calls=%async_computation.2 | async-start | bytes 4325376 | tf_op jit(solution)/shard_map/reduce_scatter | solution.py:42
  265.9 472.6 %all-reduce.3.cloned.1.call-start = ((), (), s32[]{:S(2)}) async-start(), calls=%async_computation.3 | async-start | bytes 524288 | tf_op jit(solution)/shard_map/psum | solution.py:50
Sparse Core Ops, SparseCore 0:
  10.6 143.9 all-gather.1
  266.0 213.1 reduce-scatter.1
  486.1 252.2 all-reduce.2
where the time goes:
time: 813 us; the launch traced here: 811 us
  waiting for transfers between devices  615 us (76%)
  matrix products  69.1 us (8%)
  other arithmetic  57.7 us (7%)
  local copies, waits for them, and re-layouts  54.1 us (7%)
  between operations  15.2 us (2%)
    psum x1, waiting for transfers between devices, on_device(): gram_matrix = lax.psum(gram_local, ('grp', 'col'))  257 us
    reduce_scatter x1, waiting for transfers between devices, on_device(): lax.psum_scatter(partial_slab, 'col', scatter_dimension=0, tiled=True)  213 us
    all_gather x1, waiting for transfers between devices, on_device(): piece = lax.all_gather(sketch, 'col', axis=0, tiled=True)  144 us
    dot_general x1, matrix products, on_device(): jnp.einsum('tij,tjk->tik', tile_stack, panels, precision=lax.Precision.HI...  49.4 us
    another operation x6, other arithmetic, on_device(): lower_factor = jnp.linalg.cholesky(gram_matrix)  34 us
    dot_general x1, local copies, waits for them, and re-layouts, on_device(): jnp.einsum('tij,tjk->tik', tile_stack, panels, precision=lax.Precision.HI...  24.8 us
    another operation x2, other arithmetic, on_device(): lax.linalg.triangular_solve(lower_factor, product_rows, left_side=False,...  19.7 us
    gather x1, local copies, waits for them, and re-layouts, on_device(): panels = jnp.take(panel_blocks, local_index, axis=0)  18.2 us
  transfers between devices with their start and end apart: 3, of which 3 were waited for; matrix products, arithmetic and copies ran while one was open for 0% of the time, Pallas kernels for 0%

commit v1 on v0

v1 whole, which is shorter than its diff:
```python
import jax
import jax.numpy as jnp
from jax import lax
from jax.experimental import pallas as pl
from jax.experimental.pallas import tpu as pltpu
from jax.sharding import Mesh
from jax.sharding import PartitionSpec as P

AXES = ("y", "core", "x", "z")
SIZES = (4, 2, 4, 8)
EDGE = 128
WIDTH = 256
BLOCKS = 32
BUCKETS = 32
PER_BUCKET = 6
SLOTS = 192
ROWS = 32768
GROUP = 4


def shift(value, axis, step):
    count = lax.axis_size(axis)
    return lax.ppermute(value, axis, [(i, (i + step) % count) for i in range(count)])


def ring_gather(block, axis):
    count = lax.axis_size(axis)
    found = [None] * count
    found[0] = (block,)
    behind = ahead = block
    for step in range(1, count // 2):
        behind = shift(behind, axis, 1)
        ahead = shift(ahead, axis, -1)
        found[count - step] = (behind,)
        found[step] = (ahead,)
    half = block.shape[0] // 2
    found[count // 2] = (shift(behind[:half], axis, 1), shift(ahead[half:], axis, -1))
    return found


def products_kernel(fill, blk, row, *refs):
    tiles = refs[0]
    pieces = refs[1:15]
    outs = refs[15:20]
    panels, held, total, order, tile_sem, piece_sem, out_sem = refs[20:]

    offset = 0
    piece_copies = []
    for n, piece in enumerate(pieces):
        length = piece.shape[0]
        copy = pltpu.make_async_copy(piece, panels.at[pl.ds(offset, length)], piece_sem.at[n])
        copy.start()
        piece_copies.append(copy)
        offset += length

    def tile_copy(b):
        span = pl.ds(b * PER_BUCKET, PER_BUCKET)
        return pltpu.make_async_copy(tiles.at[span], held.at[span], tile_sem.at[b])

    @pl.loop(0, BUCKETS)
    def _(b):
        tile_copy(b).start()

    def list_bucket(b, count):
        def put(j, c):
            order[c] = b * PER_BUCKET + j
            return c + 1

        return lax.fori_loop(0, fill[b], put, count)

    total[...] = jnp.zeros_like(total)

    def product(slot):
        tile = held[slot]
        panel = panels[pl.ds(pl.multiple_of(blk[slot] * EDGE, EDGE), EDGE), :]
        tile_hi = tile.astype(jnp.bfloat16)
        tile_lo = (tile - tile_hi.astype(jnp.float32)).astype(jnp.bfloat16)
        panel_hi = panel.astype(jnp.bfloat16)
        panel_lo = (panel - panel_hi.astype(jnp.float32)).astype(jnp.bfloat16)
        left = jnp.concatenate([tile_hi, tile_hi, tile_lo], axis=1)
        right = jnp.concatenate([panel_hi, panel_lo, panel_hi], axis=0)
        return jnp.dot(left, right, preferred_element_type=jnp.float32)

    for copy in piece_copies:
        copy.wait()

    def quarter(q, start):
        first = q * (BUCKETS // 4)

        @pl.loop(first, first + BUCKETS // 4)
        def _(b):
            tile_copy(b).wait()

        stop = lax.fori_loop(first, first + BUCKETS // 4, list_bucket, start)
        groups = (stop - start) // GROUP

        @pl.loop(0, groups)
        def _(g):
            slots = [order[start + g * GROUP + n] for n in range(GROUP)]
            sums = [product(s) for s in slots]
            for s, value in zip(slots, sums):
                total[row[s]] += value

        @pl.loop(start + groups * GROUP, stop)
        def _(i):
            s = order[i]
            total[row[s]] += product(s)

        return stop

    lax.fori_loop(0, 4, quarter, 0)

    offset = 0
    out_copies = []
    for n, out in enumerate(outs):
        length = out.shape[0]
        copy = pltpu.make_async_copy(total.at[pl.ds(offset, length)], out, out_sem.at[n])
        copy.start()
        out_copies.append(copy)
        offset += length
    for copy in out_copies:
        copy.wait()


def slot_products(fill, blk, row, tiles, pieces):
    block = lambda n: jax.ShapeDtypeStruct((n, EDGE, WIDTH), jnp.float32)
    any_space = pl.BlockSpec(memory_space=pl.ANY)
    smem = pl.BlockSpec(memory_space=pltpu.SMEM)
    return pl.pallas_call(
        products_kernel,
        out_shape=[block(8), block(8), block(8), block(4), block(4)],
        in_specs=[smem] * 3 + [any_space] * (1 + len(pieces)),
        out_specs=[any_space] * 5,
        scratch_shapes=[
            pltpu.VMEM((BLOCKS * 4 * EDGE, WIDTH), jnp.float32),
            pltpu.VMEM((SLOTS, EDGE, EDGE), jnp.float32),
            pltpu.VMEM((BLOCKS, EDGE, WIDTH), jnp.float32),
            pltpu.SMEM((SLOTS,), jnp.int32),
            pltpu.SemaphoreType.DMA((BUCKETS,)),
            pltpu.SemaphoreType.DMA((len(pieces),)),
            pltpu.SemaphoreType.DMA((5,)),
        ],
        compiler_params=pltpu.CompilerParams(vmem_limit_bytes=48 * 1024 * 1024),
        cost_estimate=pl.CostEstimate(
            flops=2 * 3 * SLOTS * EDGE * EDGE * WIDTH, bytes_accessed=33 * 1024 * 1024, transcendentals=0
        ),
        name="slot_products",
    )(fill, blk, row, tiles, *pieces)


BAND = 64


def factor_kernel(gram, rows, embedding, factor, work):
    work[:, :WIDTH] = gram[...]
    work[:, WIDTH:] = rows[...].T
    lane = lax.broadcasted_iota(jnp.int32, (8, EDGE), 1)
    sub = lax.broadcasted_iota(jnp.int32, (8, EDGE), 0)
    columns = (WIDTH + EDGE) // EDGE
    for band in range(WIDTH // BAND):
        top = band * BAND
        lead = top // EDGE
        strips = BAND // 8
        held = [
            [work[top + 8 * s : top + 8 * s + 8, c * EDGE : (c + 1) * EDGE] for c in range(lead, columns)]
            for s in range(strips)
        ]
        for i in range(BAND):
            s0, r = divmod(i, 8)
            at = (top + i) % EDGE
            spread = [
                jnp.broadcast_to(held[s][0][:, at : at + 1], (8, EDGE)) for s in range(s0, strips)
            ]
            pivot = jnp.broadcast_to(spread[0][r : r + 1, :], (8, EDGE))
            inverse = 1.0 / pivot
            lines = [jnp.broadcast_to(v[r : r + 1, :], (8, EDGE)) for v in held[s0]]
            scaled = [v * inverse for v in lines]
            root = lax.rsqrt(pivot)
            for s in range(s0, strips):
                weight = spread[s - s0]
                if s == s0:
                    weight = jnp.where(sub > r, weight, 0.0)
                held[s] = [v - weight * w for v, w in zip(held[s], scaled)]
            held[s0] = [jnp.where(sub == r, w * root, v) for v, w in zip(held[s0], lines)]
        for s in range(strips):
            for c in range(lead, columns):
                value = held[s][c - lead]
                if c < WIDTH // EDGE:
                    value = jnp.where(lane + c * EDGE >= sub + (top + 8 * s), value, 0.0)
                work[top + 8 * s : top + 8 * s + 8, c * EDGE : (c + 1) * EDGE] = value
        below = top + BAND
        if below < WIDTH:
            base = below // EDGE * EDGE
            left = work[top:below, base:WIDTH]
            right = work[top:below, base:]
            update = lax.dot_general(
                left,
                right,
                (((0,), (0,)), ((), ())),
                precision=lax.Precision.HIGHEST,
                preferred_element_type=jnp.float32,
            )
            work[below:, base:] -= update[below - base :, :]
    scale = jnp.sqrt(jnp.float32(ROWS))
    for band in range(WIDTH // BAND):
        top = band * BAND
        lead = top // EDGE * EDGE
        if lead:
            factor[top : top + BAND, :lead] = jnp.zeros((BAND, lead), jnp.float32)
        factor[top : top + BAND, lead:] = work[top : top + BAND, lead:WIDTH] / scale
    embedding[...] = work[:, WIDTH:].T * scale


def factor_and_solve(gram, rows):
    vmem = pl.BlockSpec(memory_space=pltpu.VMEM)
    return pl.pallas_call(
        factor_kernel,
        out_shape=[
            jax.ShapeDtypeStruct((EDGE, WIDTH), jnp.float32),
            jax.ShapeDtypeStruct((WIDTH, WIDTH), jnp.float32),
        ],
        in_specs=[vmem, vmem],
        out_specs=[vmem, vmem],
        scratch_shapes=[pltpu.VMEM((WIDTH, WIDTH + EDGE), jnp.float32)],
        compiler_params=pltpu.CompilerParams(vmem_limit_bytes=16 * 1024 * 1024),
        name="factor_and_solve",
    )(gram, rows)


def exchange(value, axes):
    return lax.all_to_all(value, axes, 0, 0, tiled=True)


def on_device(tiles, tile_rows, tile_cols, bucket_fill, row_slot, sketch):
    here_x = lax.axis_index("x")
    here_z = lax.axis_index("z")

    slot_ids = jnp.arange(SLOTS, dtype=jnp.int32)
    bucket = slot_ids // PER_BUCKET
    cols = tile_cols[0, 0]
    far_x = (bucket // 8 - here_x) % 4
    far_z = (bucket % 8 - here_z) % 8
    blk = jnp.where(
        cols < 2, far_z * 8 + far_x * 2 + cols, 64 + far_x * 16 + far_z * 2 + (cols - 2)
    )
    block_ids = jnp.arange(BLOCKS, dtype=jnp.int32)
    target = jnp.sum(
        jnp.where(tile_rows[0, 0][:, None] == block_ids[None, :], row_slot[0][None, :], 0), axis=1
    )
    ahead = (target // 8 - here_x) % 4
    chunk = jnp.where(ahead == 3, 2, jnp.where(ahead == 2, 3, ahead))
    row = chunk * 8 + target % 8

    with jax.named_scope("gather"):
        half = sketch.shape[0] // 2
        along_x = ring_gather(sketch[:half], "x")
        along_z = ring_gather(sketch[half:], "z")
        slab = jnp.concatenate([part for block in along_x for part in block], axis=0)
        line = jnp.concatenate([part for block in along_z for part in block], axis=0)
        first = ring_gather(slab, "z")
        second = ring_gather(line, "x")
        pieces = [part for block in first + second for part in block]

    sums = slot_products(bucket_fill[0, 0], blk, row, tiles[0, 0], pieces)

    with jax.named_scope("scatter_rows"):
        own, up, down, far_up, far_down = sums
        from_below = shift(far_up, "x", 1)
        from_above = shift(far_down, "x", -1)
        up = jnp.concatenate([up[:4] + from_below, up[4:]], axis=0)
        down = jnp.concatenate([down[:4], down[4:] + from_above], axis=0)
        own = own + shift(up, "x", 1) + shift(down, "x", -1)
        product_rows = jnp.sum(exchange(own, "z"), axis=0)

    with jax.named_scope("gram"):
        gram = jnp.dot(
            product_rows.T,
            product_rows,
            precision=lax.Precision.HIGHEST,
            preferred_element_type=jnp.float32,
        )
        ring = ("y", "core", "x")
        part = jnp.sum(exchange(gram, ring).reshape(32, 8, WIDTH), axis=0)
        part = jnp.sum(
            exchange(jnp.broadcast_to(part[None], (8, 8, WIDTH)), "z"), axis=0
        )
        gram = exchange(jnp.broadcast_to(part[None], (32, 8, WIDTH)), ring).reshape(WIDTH, WIDTH)

    embedding, factor = factor_and_solve(gram, product_rows)
    return embedding, factor


def solution(mesh):
    fine = Mesh(mesh.devices.reshape(SIZES), AXES)
    grp, col = ("y", "core"), ("x", "z")
    placed = (
        P(grp, col, None, None, None),
        P(grp, col, None),
        P(grp, col, None),
        P(grp, col, None),
        P(grp, None),
        P(col, None),
    )
    return jax.shard_map(
        on_device,
        mesh=fine,
        in_specs=placed,
        out_specs=(P(AXES, None), P()),
        check_vma=False,
    )
```

time: 813 us -> 287 us (0.35)
  waiting for transfers between devices: 615 us -> 108 us
  blocking collectives: 0 us -> 74.5 us
  matrix products: 69.1 us -> 0.37 us
  other arithmetic: 57.7 us -> 0.79 us
  Pallas kernels: 0 us -> 53.9 us
  local copies, waits for them, and re-layouts: 54.1 us -> 4.62 us
  starting transfers between devices: 0.34 us -> 43.7 us
  between operations: 15.2 us -> 1 us
    psum x1 -> x0, waiting for transfers between devices: 257 us -> none  [on_device(): gram_matrix = lax.psum(gram_local, ('grp', 'col'))]
    reduce_scatter x1 -> x0, waiting for transfers between devices: 213 us -> none  [on_device(): lax.psum_scatter(partial_slab, 'col', scatter_dimension=0, tiled=True)]
    all_gather x1 -> x0, waiting for transfers between devices: 144 us -> none  [on_device(): piece = lax.all_gather(sketch, 'col', axis=0, tiled=True)]
    ppermute x0 -> x28, waiting for transfers between devices: none -> 108 us  [shift(): lax.ppermute(value, axis, [(i, (i + step) % count) for i in range(count)])]
    all_to_all x0 -> x4, blocking collectives: none -> 74.5 us  [exchange(): return lax.all_to_all(value, axes, 0, 0, tiled=True)]
    dot_general x2 -> x0, matrix products: 64 us -> none  [the longest x1 49.4 us: on_device(): jnp.einsum('tij,tjk->tik', tile_stack, panels, precision=lax.Precision.HI...]
    pallas_call x0 -> x2, Pallas kernels: none -> 53.9 us  [the longest x1 35.3 us: factor_and_solve(): pl.pallas_call(factor_kernel, out_shape=[jax.ShapeDtypeStruct((EDGE, WIDT...]
    another operation x8 -> x0, other arithmetic: 53.7 us -> none  [the longest x6 34 us: on_device(): lower_factor = jnp.linalg.cholesky(gram_matrix)]
  transfers between devices with their start and end apart: 3 -> 28, of which waited for: 3 -> 14; matrix products, arithmetic and copies ran while one was open for 0% -> 1% of each run, Pallas kernels for 0% -> 0%
where the time goes in v1:
time: 287 us
  waiting for transfers between devices  108 us (38%)
  blocking collectives  74.5 us (26%)
  Pallas kernels  53.9 us (19%)
  starting transfers between devices  43.7 us (15%)
  local copies, waits for them, and re-layouts  4.62 us (2%)
    ppermute x28, waiting for transfers between devices, shift(): lax.ppermute(value, axis, [(i, (i + step) % count) for i in range(count)])  108 us
    all_to_all x4, blocking collectives, exchange(): return lax.all_to_all(value, axes, 0, 0, tiled=True)  74.5 us
    ppermute x28, starting transfers between devices, shift(): lax.ppermute(value, axis, [(i, (i + step) % count) for i in range(count)])  43.7 us
    pallas_call x1, Pallas kernels, factor_and_solve(): pl.pallas_call(factor_kernel, out_shape=[jax.ShapeDtypeStruct((EDGE, WIDT...  35.3 us
    pallas_call x1, Pallas kernels, slot_products(): pl.pallas_call(products_kernel, out_shape=[block(8), block(8), block(8),...  18.6 us
  transfers between devices with their start and end apart: 28, of which 14 were waited for; matrix products, arithmetic and copies ran while one was open for 1% of the time, Pallas kernels for 0%

profile of v1, /device:TPU:1, one launch (start us, length us, event | category | flops | bytes accessed | tf_op | source)
XLA Modules:
  0.0 286.6 jit_solution(7478257879054007675)
XLA Ops:
  0.6 1.1 fusion.10
  1.7 2.5 collective-permute-start.15
  4.3 1.2 collective-permute-start.1
  5.5 1.5 collective-permute-start
  7.0 4.0 %collective-permute-start.12 = (f32[256,256]{1,0:T(8,128)S(1)}, f32[256,256]{1,0:T(8,128)S(1)}, u32[]{:S(2)}, u32[]{:S(2)}) collective-permute-start(f32[256,256]{1,0:T(8,128)S(1)} %get-tuple-element.16), channel_id=1, source_target_pairs={{0,7},{1,0},{2,1},{3,2},{4,3},{5,4},{6,5},{7,6},{8,15},{9,8},{10,9... | collective-permute-start | bytes 786440 | tf_op jit(solution)/shard_map/gather/ppermute | solution.py:23
  11.0 3.3 %collective-permute-done.15 = f32[256,256]{1,0:T(8,128)S(1)} collective-permute-done((f32[256,256]{1,0:T(8,128)S(1)}, f32[256,256]{1,0:T(8,128)S(1)}, u32[]{:S(2)}, u32[]{:S(2)}) %collective-permute-start.15) | collective-permute-done | bytes 262176 | tf_op jit(solution)/shard_map/gather/ppermute | solution.py:23
  14.2 0.0 collective-permute-start.16
  14.3 0.0 collective-permute-done.1
  14.3 1.3 collective-permute-start.2
  15.6 0.0 collective-permute-done
  15.6 1.5 collective-permute-start.3
  17.1 0.0 collective-permute-done.12
  17.1 2.7 collective-permute-start.13
  19.8 2.2 collective-permute-done.16
  22.0 0.0 collective-permute-start.17
  22.1 1.3 collective-permute-done.13
  23.3 3.4 %collective-permute-start.14 = (f32[256,256]{1,0:T(8,128)S(1)}, f32[256,256]{1,0:T(8,128)S(1)}, u32[]{:S(2)}, u32[]{:S(2)}) collective-permute-start(f32[256,256]{1,0:T(8,128)S(1)} %collective-permute-done.13), channel_id=1, source_target_pairs={{0,7},{1,0},{2,1},{3,2},{4,3},{5,4},{6,5},{7,6},{8,15},{9,8},{10,9... | collective-permute-start | bytes 786440 | tf_op jit(solution)/shard_map/gather/ppermute | solution.py:23
  26.8 0.1 collective-permute-start.7
  26.9 2.7 collective-permute-start.4
  29.6 0.1 collective-permute-start.18
  29.7 0.4 collective-permute-done.14
  30.1 3.2 %collective-permute-start.19 = (f32[128,256]{1,0:T(8,128)S(1)}, f32[128,256]{1,0:T(8,128)S(1)}, u32[]{:S(2)}, u32[]{:S(2)}) collective-permute-start(f32[128,256]{1,0:T(8,128)S(1)} %slice.61), channel_id=1, source_target_pairs={{0,7},{1,0},{2,1},{3,2},{4,3},{5,4},{6,5},{7,6},{8,15},{9,8},{10,9... | collective-permute-start | bytes 393224 | tf_op jit(solution)/shard_map/gather/ppermute | solution.py:23
  33.3 20.5 %collective-permute-done.18 = f32[128,256]{1,0:T(8,128)S(1)} collective-permute-done((f32[128,256]{1,0:T(8,128)S(1)}, f32[128,256]{1,0:T(8,128)S(1)}, u32[]{:S(2)}, u32[]{:S(2)}) %collective-permute-start.18) | collective-permute-done | bytes 131104 | tf_op jit(solution)/shard_map/gather/ppermute | solution.py:23
  53.8 1.1 collective-permute-done.19
  55.1 1.2 collective-permute-start.21
  56.3 1.5 collective-permute-start.20
  57.8 0.0 collective-permute-done.4.refs_2_
  57.9 3.3 %collective-permute-start.5 = (f32[1024,256]{1,0:T(8,128)S(1)}, f32[1024,256]{1,0:T(8,128)S(1)}, u32[]{:S(2)}, u32[]{:S(2)}) collective-permute-start(f32[1024,256]{1,0:T(8,128)S(1)} %collective-permute-done.4.refs_2_), channel_id=1, source_target_pairs={{0,7},{1,0},{2,1},{3,2},{4,3},{5,4},{6,5},{7,6},{8,15},{9,8},{10,9... | collective-permute-start | bytes 3145736 | tf_op jit(solution)/shard_map/gather/ppermute | solution.py:23
  61.1 19.0 %collective-permute-done.8.refs_8_ = f32[1024,256]{1,0:T(8,128)S(1)} collective-permute-done((f32[1024,256]{1,0:T(8,128)S(1)}, f32[1024,256]{1,0:T(8,128)S(1)}, u32[]{:S(2)}, u32[]{:S(2)}) %collective-permute-start.8) | collective-permute-done | bytes 1048608 | tf_op jit(solution)/shard_map/gather/ppermute | solution.py:23
  80.2 2.7 collective-permute-start.6
  82.9 17.0 %collective-permute-done.21.refs_14_ = f32[2048,256]{1,0:T(8,128)S(1)} collective-permute-done((f32[2048,256]{1,0:T(8,128)S(1)}, f32[2048,256]{1,0:T(8,128)S(1)}, u32[]{:S(2)}, u32[]{:S(2)}) %collective-permute-start.21) | collective-permute-done | bytes 2097184 | tf_op jit(solution)/shard_map/gather/ppermute | solution.py:23
  99.9 1.1 slice.62
  101.0 1.2 collective-permute-start.22
  102.2 0.0 collective-permute-done.20.refs_11_
  102.2 1.1 slice.63
  103.3 1.6 collective-permute-start.23
  104.9 0.0 collective-permute-done.9.refs_7_
  104.9 0.9 slice.58
  105.8 3.1 %collective-permute-start.11 = (f32[512,256]{1,0:T(8,128)S(1)}, f32[512,256]{1,0:T(8,128)S(1)}, u32[]{:S(2)}, u32[]{:S(2)}) collective-permute-start(f32[512,256]{1,0:T(8,128)S(1)} %slice.59), channel_id=1, source_target_pairs={{0,7},{1,0},{2,1},{3,2},{4,3},{5,4},{6,5},{7,6},{8,15},{9,8},{10,9... | collective-permute-start | bytes 1572872 | tf_op jit(solution)/shard_map/gather/ppermute | solution.py:23
  109.0 0.1 select_reduce_fusion
  109.1 6.9 %collective-permute-done.10.refs_5_ = f32[512,256]{1,0:T(8,128)S(1)} collective-permute-done((f32[512,256]{1,0:T(8,128)}, f32[512,256]{1,0:T(8,128)S(1)}, u32[]{:S(2)}, u32[]{:S(2)}) %collective-permute-start.10) | collective-permute-done | bytes 524320 | tf_op jit(solution)/shard_map/gather/ppermute | solution.py:23
  116.0 6.7 %collective-permute-done.22.refs_12_ = f32[1024,256]{1,0:T(8,128)} collective-permute-done((f32[1024,256]{1,0:T(8,128)}, f32[1024,256]{1,0:T(8,128)}, u32[]{:S(2)}, u32[]{:S(2)}) %collective-permute-start.22) | collective-permute-done | bytes 1048608 | tf_op jit(solution)/shard_map/gather/ppermute | solution.py:23
  122.8 1.9 collective-permute-done.23.refs_13_
  124.6 18.6 %slot_products.1 = (f32[8,128,256]{2,1,0:T(8,128)S(1)}, f32[8,128,256]{2,1,0:T(8,128)S(1)}, f32[8,128,256]{2,1,0:T(8,128)S(1)}, f32[4,128,256]{2,1,0:T(8,128)S(1)}, f32[4,128,256]{2,1,0:T(8,128)S(1)}) custom-call(s32[32]{0:T(128)S(1)} %bitcast.15, s32[192]{0:T(256)S(1)} %get-tuple-element.20.blk, s32[192]{0:T(256)S(1)} %get-tuple-element.21.row, ...), custom_call_target="tpu_custom_call" | custom-call | flops 4831838208 | bytes 34603008 | tf_op jit(solution)/shard_map/slot_products/pallas_call | solution.py:129
  143.2 1.8 collective-permute-start.26
  145.0 0.0 collective-permute-start.24
  145.0 6.3 %collective-permute-done.26 = f32[4,128,256]{2,1,0:T(8,128)S(1)} collective-permute-done((f32[4,128,256]{2,1,0:T(8,128)S(1)}, f32[4,128,256]{2,1,0:T(8,128)S(1)}, u32[]{:S(2)}, u32[]{:S(2)}) %collective-permute-start.26) | collective-permute-done | bytes 524320 | tf_op jit(solution)/shard_map/scatter_rows/ppermute | solution.py:23
  151.3 0.1 fusion.9
  151.4 0.1 pad_maximum_fusion.1
  151.5 3.0 %collective-permute-start.27 = (f32[8,128,256]{2,1,0:T(8,128)S(1)}, f32[8,128,256]{2,1,0:T(8,128)S(1)}, u32[]{:S(2)}, u32[]{:S(2)}) collective-permute-start(f32[8,128,256]{2,1,0:T(8,128)S(1)} %pad_maximum_fusion.1), channel_id=1, source_target_pairs={{0,24},{8,0},{16,8},{24,16},{1,25},{9,1},{17,9},{25,17},{2,26},{10... | collective-permute-start | bytes 3145736 | tf_op jit(solution)/shard_map/scatter_rows/ppermute | solution.py:23
  154.5 0.1 slice_add_fusion.1
  154.6 0.1 pad_maximum_fusion
  154.7 0.1 collective-permute-start.25
  154.8 17.7 %collective-permute-done.27 = f32[8,128,256]{2,1,0:T(8,128)S(1)} collective-permute-done((f32[8,128,256]{2,1,0:T(8,128)S(1)}, f32[8,128,256]{2,1,0:T(8,128)S(1)}, u32[]{:S(2)}, u32[]{:S(2)}) %collective-permute-start.27) | collective-permute-done | bytes 1048608 | tf_op jit(solution)/shard_map/scatter_rows/ppermute | solution.py:23
  172.5 3.4 %collective-permute-done.25 = f32[8,128,256]{2,1,0:T(8,128)S(1)} collective-permute-done((f32[8,128,256]{2,1,0:T(8,128)S(1)}, f32[8,128,256]{2,1,0:T(8,128)S(1)}, u32[]{:S(2)}, u32[]{:S(2)}) %collective-permute-start.25) | collective-permute-done | bytes 1048608 | tf_op jit(solution)/shard_map/scatter_rows/ppermute | solution.py:23
  175.9 0.2 add_add_fusion
  176.1 23.1 %all_to_all.21 = f32[8,128,256]{2,1,0:T(8,128)S(1)} all-to-all(f32[8,128,256]{2,1,0:T(8,128)S(1)} %add_add_fusion), channel_id=1, replica_groups=mesh['y'=4,'core'=2,'x'=4,'z'=8] {'z'}, dimensions={0} | all-to-all | bytes 2097152 | tf_op jit(solution)/shard_map/scatter_rows/all_to_all | solution.py:231
  199.2 0.1 reduce_sum.37.rows
  199.3 0.1 copy.10
  199.4 0.4 fusion
  199.8 27.8 %all_to_all.22 = f32[32,8,256]{2,1,0:T(8,128)S(1)} all-to-all(f32[32,8,256]{2,1,0:T(8,128)S(1)} %fusion), channel_id=1, replica_groups=mesh['y'=4,'core'=2,'x'=4,'z'=8] {'y','core','x'}, dimensions={0} | all-to-all | bytes 524288 | tf_op jit(solution)/shard_map/gram/all_to_all | solution.py:231
  227.7 9.5 %all_to_all.23 = f32[8,8,256]{2,1,0:T(8,128)S(1)} all-to-all(f32[8,8,256]{2,1,0:T(8,128)S(1)} %broadcast_in_dim.33), channel_id=1, replica_groups=mesh['y'=4,'core'=2,'x'=4,'z'=8] {'z'}, dimensions={0} | all-to-all | bytes 131072 | tf_op jit(solution)/shard_map/gram/all_to_all | solution.py:231
  237.2 14.0 %all_to_all.24 = f32[32,8,256]{2,1,0:T(8,128)S(1)} all-to-all(f32[32,8,256]{2,1,0:T(8,128)S(1)} %broadcast_in_dim.34), channel_id=1, replica_groups=mesh['y'=4,'core'=2,'x'=4,'z'=8] {'y','core','x'}, dimensions={0} | all-to-all | bytes 524288 | tf_op jit(solution)/shard_map/gram/all_to_all | solution.py:231
  251.3 35.3 %factor_and_solve.1 = (f32[128,256]{1,0:T(8,128)}, f32[256,256]{1,0:T(8,128)}) custom-call(f32[256,256]{1,0:T(8,128)S(1)} %bitcast.14, f32[128,256]{1,0:T(8,128)S(1)} %reduce_sum.37.rows), custom_call_target="tpu_custom_call" | custom-call | tf_op jit(solution)/shard_map/factor_and_solve/pallas_call | solution.py:216
  (61 shorter events, 0.5 us)
Async XLA Ops:
  1.7 12.5 %collective-permute-start.15 = (f32[256,256]{1,0:T(8,128)S(1)}, f32[256,256]{1,0:T(8,128)S(1)}, u32[]{:S(2)}, u32[]{:S(2)}) collective-permute-start(f32[256,256]{1,0:T(8,128)S(1)} %get-tuple-element.16), channel_id=1, source_target_pairs={{0,1},{1,2},{2,3},{3,4},{4,5},{5,6},{6,7},{7,0},{8,9},{9,10},{10,1... | collective-permute-start | bytes 786440 | tf_op jit(solution)/shard_map/gather/ppermute | solution.py:23
  4.3 10.0 %collective-permute-start.1 = (f32[256,256]{1,0:T(8,128)S(1)}, f32[256,256]{1,0:T(8,128)S(1)}, u32[]{:S(2)}, u32[]{:S(2)}) collective-permute-start(f32[256,256]{1,0:T(8,128)S(1)} %get-tuple-element.19), channel_id=1, source_target_pairs={{0,8},{8,16},{16,24},{24,0},{1,9},{9,17},{17,25},{25,1},{2,10},{10... | collective-permute-start | bytes 786440 | tf_op jit(solution)/shard_map/gather/ppermute | solution.py:23
  5.5 10.1 %collective-permute-start = (f32[256,256]{1,0:T(8,128)S(1)}, f32[256,256]{1,0:T(8,128)S(1)}, u32[]{:S(2)}, u32[]{:S(2)}) collective-permute-start(f32[256,256]{1,0:T(8,128)S(1)} %get-tuple-element.19), channel_id=1, source_target_pairs={{0,24},{8,0},{16,8},{24,16},{1,25},{9,1},{17,9},{25,17},{2,26},{10... | collective-permute-start | bytes 786440 | tf_op jit(solution)/shard_map/gather/ppermute | solution.py:23
  7.0 10.2 %collective-permute-start.12 = (f32[256,256]{1,0:T(8,128)S(1)}, f32[256,256]{1,0:T(8,128)S(1)}, u32[]{:S(2)}, u32[]{:S(2)}) collective-permute-start(f32[256,256]{1,0:T(8,128)S(1)} %get-tuple-element.16), channel_id=1, source_target_pairs={{0,7},{1,0},{2,1},{3,2},{4,3},{5,4},{6,5},{7,6},{8,15},{9,8},{10,9... | collective-permute-start | bytes 786440 | tf_op jit(solution)/shard_map/gather/ppermute | solution.py:23
  14.2 7.8 %collective-permute-start.16 = (f32[256,256]{1,0:T(8,128)S(1)}, f32[256,256]{1,0:T(8,128)S(1)}, u32[]{:S(2)}, u32[]{:S(2)}) collective-permute-start(f32[256,256]{1,0:T(8,128)S(1)} %collective-permute-done.15), channel_id=1, source_target_pairs={{0,1},{1,2},{2,3},{3,4},{4,5},{5,6},{6,7},{7,0},{8,9},{9,10},{10,1... | collective-permute-start | bytes 786440 | tf_op jit(solution)/shard_map/gather/ppermute | solution.py:23
  14.3 7.8 %collective-permute-start.2 = (f32[128,256]{1,0:T(8,128)S(1)}, f32[128,256]{1,0:T(8,128)S(1)}, u32[]{:S(2)}, u32[]{:S(2)}) collective-permute-start(f32[128,256]{1,0:T(8,128)S(1)} %slice.56), channel_id=1, source_target_pairs={{0,8},{8,16},{16,24},{24,0},{1,9},{9,17},{17,25},{25,1},{2,10},{10... | collective-permute-start | bytes 393224 | tf_op jit(solution)/shard_map/gather/ppermute | solution.py:23
  15.6 11.2 %collective-permute-start.3 = (f32[128,256]{1,0:T(8,128)S(1)}, f32[128,256]{1,0:T(8,128)S(1)}, u32[]{:S(2)}, u32[]{:S(2)}) collective-permute-start(f32[128,256]{1,0:T(8,128)S(1)} %slice.57), channel_id=1, source_target_pairs={{0,24},{8,0},{16,8},{24,16},{1,25},{9,1},{17,9},{25,17},{2,26},{10... | collective-permute-start | bytes 393224 | tf_op jit(solution)/shard_map/gather/ppermute | solution.py:23
  17.1 6.2 %collective-permute-start.13 = (f32[256,256]{1,0:T(8,128)S(1)}, f32[256,256]{1,0:T(8,128)S(1)}, u32[]{:S(2)}, u32[]{:S(2)}) collective-permute-start(f32[256,256]{1,0:T(8,128)S(1)} %collective-permute-done.12), channel_id=1, source_target_pairs={{0,7},{1,0},{2,1},{3,2},{4,3},{5,4},{6,5},{7,6},{8,15},{9,8},{10,9... | collective-permute-start | bytes 786440 | tf_op jit(solution)/shard_map/gather/ppermute | solution.py:23
  22.0 7.5 %collective-permute-start.17 = (f32[256,256]{1,0:T(8,128)S(1)}, f32[256,256]{1,0:T(8,128)S(1)}, u32[]{:S(2)}, u32[]{:S(2)}) collective-permute-start(f32[256,256]{1,0:T(8,128)S(1)} %collective-permute-done.16), channel_id=1, source_target_pairs={{0,1},{1,2},{2,3},{3,4},{4,5},{5,6},{6,7},{7,0},{8,9},{9,10},{10,1... | collective-permute-start | bytes 786440 | tf_op jit(solution)/shard_map/gather/ppermute | solution.py:23
  23.3 6.7 %collective-permute-start.14 = (f32[256,256]{1,0:T(8,128)S(1)}, f32[256,256]{1,0:T(8,128)S(1)}, u32[]{:S(2)}, u32[]{:S(2)}) collective-permute-start(f32[256,256]{1,0:T(8,128)S(1)} %collective-permute-done.13), channel_id=1, source_target_pairs={{0,7},{1,0},{2,1},{3,2},{4,3},{5,4},{6,5},{7,6},{8,15},{9,8},{10,9... | collective-permute-start | bytes 786440 | tf_op jit(solution)/shard_map/gather/ppermute | solution.py:23
  26.8 53.4 %copy-start.6 = (f32[1024,256]{1,0:T(8,128)}, f32[1024,256]{1,0:T(8,128)S(1)}, u32[]{:S(2)}) copy-start(f32[1024,256]{1,0:T(8,128)S(1)} %constant_dynamic-update-slice_fusion.refs_1_) | copy-start | bytes 3145732
  26.8 31.0 %collective-permute-start.7 = (f32[1024,256]{1,0:T(8,128)S(1)}, f32[1024,256]{1,0:T(8,128)S(1)}, u32[]{:S(2)}, u32[]{:S(2)}) collective-permute-start(f32[1024,256]{1,0:T(8,128)S(1)} %constant_dynamic-update-slice_fusion.refs_1_), channel_id=1, source_target_pairs={{0,1},{1,2},{2,3},{3,4},{4,5},{5,6},{6,7},{7,0},{8,9},{9,10},{10,1... | collective-permute-start | bytes 3145736 | tf_op jit(solution)/shard_map/gather/ppermute | solution.py:23
  26.9 31.0 %collective-permute-start.4 = (f32[1024,256]{1,0:T(8,128)S(1)}, f32[1024,256]{1,0:T(8,128)S(1)}, u32[]{:S(2)}, u32[]{:S(2)}) collective-permute-start(f32[1024,256]{1,0:T(8,128)S(1)} %constant_dynamic-update-slice_fusion.refs_1_), channel_id=1, source_target_pairs={{0,7},{1,0},{2,1},{3,2},{4,3},{5,4},{6,5},{7,6},{8,15},{9,8},{10,9... | collective-permute-start | bytes 3145736 | tf_op jit(solution)/shard_map/gather/ppermute | solution.py:23
  29.6 24.3 %collective-permute-start.18 = (f32[128,256]{1,0:T(8,128)S(1)}, f32[128,256]{1,0:T(8,128)S(1)}, u32[]{:S(2)}, u32[]{:S(2)}) collective-permute-start(f32[128,256]{1,0:T(8,128)S(1)} %slice.60), channel_id=1, source_target_pairs={{0,1},{1,2},{2,3},{3,4},{4,5},{5,6},{6,7},{7,0},{8,9},{9,10},{10,1... | collective-permute-start | bytes 393224 | tf_op jit(solution)/shard_map/gather/ppermute | solution.py:23
  30.1 24.9 %collective-permute-start.19 = (f32[128,256]{1,0:T(8,128)S(1)}, f32[128,256]{1,0:T(8,128)S(1)}, u32[]{:S(2)}, u32[]{:S(2)}) collective-permute-start(f32[128,256]{1,0:T(8,128)S(1)} %slice.61), channel_id=1, source_target_pairs={{0,7},{1,0},{2,1},{3,2},{4,3},{5,4},{6,5},{7,6},{8,15},{9,8},{10,9... | collective-permute-start | bytes 393224 | tf_op jit(solution)/shard_map/gather/ppermute | solution.py:23
  55.0 53.9 %copy-start.3 = (f32[2048,256]{1,0:T(8,128)}, f32[2048,256]{1,0:T(8,128)S(1)}, u32[]{:S(2)}) copy-start(f32[2048,256]{1,0:T(8,128)S(1)} %constant_dynamic-update-slice_fusion.5.refs_10_) | copy-start | bytes 6291460
  55.1 44.8 %collective-permute-start.21 = (f32[2048,256]{1,0:T(8,128)S(1)}, f32[2048,256]{1,0:T(8,128)S(1)}, u32[]{:S(2)}, u32[]{:S(2)}) collective-permute-start(f32[2048,256]{1,0:T(8,128)S(1)} %constant_dynamic-update-slice_fusion.5.refs_10_), channel_id=1, source_target_pairs={{0,8},{8,16},{16,24},{24,0},{1,9},{9,17},{17,25},{25,1},{2,10},{10... | collective-permute-start | bytes 6291464 | tf_op jit(solution)/shard_map/gather/ppermute | solution.py:23
  56.3 45.9 %collective-permute-start.20 = (f32[2048,256]{1,0:T(8,128)S(1)}, f32[2048,256]{1,0:T(8,128)S(1)}, u32[]{:S(2)}, u32[]{:S(2)}) collective-permute-start(f32[2048,256]{1,0:T(8,128)S(1)} %constant_dynamic-update-slice_fusion.5.refs_10_), channel_id=1, source_target_pairs={{0,24},{8,0},{16,8},{24,16},{1,25},{9,1},{17,9},{25,17},{2,26},{10... | collective-permute-start | bytes 6291464 | tf_op jit(solution)/shard_map/gather/ppermute | solution.py:23
  57.8 25.1 %copy-start.7 = (f32[1024,256]{1,0:T(8,128)}, f32[1024,256]{1,0:T(8,128)S(1)}, u32[]{:S(2)}) copy-start(f32[1024,256]{1,0:T(8,128)S(1)} %collective-permute-done.7.refs_9_) | copy-start | bytes 3145732
  57.8 22.3 %collective-permute-start.8 = (f32[1024,256]{1,0:T(8,128)S(1)}, f32[1024,256]{1,0:T(8,128)S(1)}, u32[]{:S(2)}, u32[]{:S(2)}) collective-permute-start(f32[1024,256]{1,0:T(8,128)S(1)} %collective-permute-done.7.refs_9_), channel_id=1, source_target_pairs={{0,1},{1,2},{2,3},{3,4},{4,5},{5,6},{6,7},{7,0},{8,9},{9,10},{10,1... | collective-permute-start | bytes 3145736 | tf_op jit(solution)/shard_map/gather/ppermute | solution.py:23
  57.8 22.3 %copy-start.8 = (f32[1024,256]{1,0:T(8,128)}, f32[1024,256]{1,0:T(8,128)S(1)}, u32[]{:S(2)}) copy-start(f32[1024,256]{1,0:T(8,128)S(1)} %collective-permute-done.4.refs_2_) | copy-start | bytes 3145732
  57.9 22.3 %collective-permute-start.5 = (f32[1024,256]{1,0:T(8,128)S(1)}, f32[1024,256]{1,0:T(8,128)S(1)}, u32[]{:S(2)}, u32[]{:S(2)}) collective-permute-start(f32[1024,256]{1,0:T(8,128)S(1)} %collective-permute-done.4.refs_2_), channel_id=1, source_target_pairs={{0,7},{1,0},{2,1},{3,2},{4,3},{5,4},{6,5},{7,6},{8,15},{9,8},{10,9... | collective-permute-start | bytes 3145736 | tf_op jit(solution)/shard_map/gather/ppermute | solution.py:23
  80.1 28.8 %copy-start.9 = (f32[1024,256]{1,0:T(8,128)}, f32[1024,256]{1,0:T(8,128)S(1)}, u32[]{:S(2)}) copy-start(f32[1024,256]{1,0:T(8,128)S(1)} %collective-permute-done.8.refs_8_) | copy-start | bytes 3145732
  80.1 24.7 %collective-permute-start.9 = (f32[1024,256]{1,0:T(8,128)S(1)}, f32[1024,256]{1,0:T(8,128)S(1)}, u32[]{:S(2)}, u32[]{:S(2)}) collective-permute-start(f32[1024,256]{1,0:T(8,128)S(1)} %collective-permute-done.8.refs_8_), channel_id=1, source_target_pairs={{0,1},{1,2},{2,3},{3,4},{4,5},{5,6},{6,7},{7,0},{8,9},{9,10},{10,1... | collective-permute-start | bytes 3145736 | tf_op jit(solution)/shard_map/gather/ppermute | solution.py:23
  80.2 28.7 %copy-start.10 = (f32[1024,256]{1,0:T(8,128)}, f32[1024,256]{1,0:T(8,128)S(1)}, u32[]{:S(2)}) copy-start(f32[1024,256]{1,0:T(8,128)S(1)} %collective-permute-done.5.refs_3_) | copy-start | bytes 3145732
  80.2 25.6 %collective-permute-start.6 = (f32[1024,256]{1,0:T(8,128)S(1)}, f32[1024,256]{1,0:T(8,128)S(1)}, u32[]{:S(2)}, u32[]{:S(2)}) collective-permute-start(f32[1024,256]{1,0:T(8,128)S(1)} %collective-permute-done.5.refs_3_), channel_id=1, source_target_pairs={{0,7},{1,0},{2,1},{3,2},{4,3},{5,4},{6,5},{7,6},{8,15},{9,8},{10,9... | collective-permute-start | bytes 3145736 | tf_op jit(solution)/shard_map/gather/ppermute | solution.py:23
  99.9 5.9 %copy-start.1 = (f32[2048,256]{1,0:T(8,128)}, f32[2048,256]{1,0:T(8,128)S(1)}, u32[]{:S(2)}) copy-start(f32[2048,256]{1,0:T(8,128)S(1)} %collective-permute-done.21.refs_14_) | copy-start | bytes 6291460
  101.0 7.9 %copy-start.12 = (s32[1,1,192]{2,1,0:T(1,128)S(1)}, s32[1,1,192]{2,1,0:T(1,128)}, u32[]{:S(2)}) copy-start(s32[1,1,192]{2,1,0:T(1,128)} %param.7) | copy-start | bytes 2308
  101.0 8.0 %copy-start.13 = (s32[1,32]{1,0:T(1,128)S(1)}, s32[1,32]{1,0:T(1,128)}, u32[]{:S(2)}) copy-start(s32[1,32]{1,0:T(1,128)} %param.10) | copy-start | bytes 388
  101.0 8.0 %copy-start.11 = (s32[1,1,192]{2,1,0:T(1,128)S(1)}, s32[1,1,192]{2,1,0:T(1,128)}, u32[]{:S(2)}) copy-start(s32[1,1,192]{2,1,0:T(1,128)} %param.8) | copy-start | bytes 2308
  101.0 23.6 %copy-start = (s32[1,1,32]{2,1,0:T(1,128)S(1)}, s32[1,1,32]{2,1,0:T(1,128)}, u32[]{:S(2)}) copy-start(s32[1,1,32]{2,1,0:T(1,128)} %param.9) | copy-start | bytes 388
  101.0 21.7 %collective-permute-start.22 = (f32[1024,256]{1,0:T(8,128)}, f32[1024,256]{1,0:T(8,128)}, u32[]{:S(2)}, u32[]{:S(2)}) collective-permute-start(f32[1024,256]{1,0:T(8,128)} %slice.62), channel_id=1, source_target_pairs={{0,8},{8,16},{16,24},{24,0},{1,9},{9,17},{17,25},{25,1},{2,10},{10... | collective-permute-start | bytes 3145736 | tf_op jit(solution)/shard_map/gather/ppermute | solution.py:23
  102.2 3.6 %copy-start.2 = (f32[2048,256]{1,0:T(8,128)}, f32[2048,256]{1,0:T(8,128)S(1)}, u32[]{:S(2)}) copy-start(f32[2048,256]{1,0:T(8,128)S(1)} %collective-permute-done.20.refs_11_) | copy-start | bytes 6291460
  103.3 21.3 %collective-permute-start.23 = (f32[1024,256]{1,0:T(8,128)}, f32[1024,256]{1,0:T(8,128)}, u32[]{:S(2)}, u32[]{:S(2)}) collective-permute-start(f32[1024,256]{1,0:T(8,128)} %slice.63), channel_id=1, source_target_pairs={{0,24},{8,0},{16,8},{24,16},{1,25},{9,1},{17,9},{25,17},{2,26},{10... | collective-permute-start | bytes 3145736 | tf_op jit(solution)/shard_map/gather/ppermute | solution.py:23
  104.9 4.0 %copy-start.4 = (f32[1024,256]{1,0:T(8,128)}, f32[1024,256]{1,0:T(8,128)S(1)}, u32[]{:S(2)}) copy-start(f32[1024,256]{1,0:T(8,128)S(1)} %collective-permute-done.9.refs_7_) | copy-start | bytes 3145732
  105.8 10.3 %collective-permute-start.10 = (f32[512,256]{1,0:T(8,128)}, f32[512,256]{1,0:T(8,128)S(1)}, u32[]{:S(2)}, u32[]{:S(2)}) collective-permute-start(f32[512,256]{1,0:T(8,128)} %slice.58), channel_id=1, source_target_pairs={{0,1},{1,2},{2,3},{3,4},{4,5},{5,6},{6,7},{7,0},{8,9},{9,10},{10,1... | collective-permute-start | bytes 1572872 | tf_op jit(solution)/shard_map/gather/ppermute | solution.py:23
  105.8 3.2 %copy-start.5 = (f32[1024,256]{1,0:T(8,128)}, f32[1024,256]{1,0:T(8,128)S(1)}, u32[]{:S(2)}) copy-start(f32[1024,256]{1,0:T(8,128)S(1)} %collective-permute-done.6.refs_4_) | copy-start | bytes 3145732
  105.8 10.2 %collective-permute-start.11 = (f32[512,256]{1,0:T(8,128)S(1)}, f32[512,256]{1,0:T(8,128)S(1)}, u32[]{:S(2)}, u32[]{:S(2)}) collective-permute-start(f32[512,256]{1,0:T(8,128)S(1)} %slice.59), channel_id=1, source_target_pairs={{0,7},{1,0},{2,1},{3,2},{4,3},{5,4},{6,5},{7,6},{8,15},{9,8},{10,9... | collective-permute-start | bytes 1572872 | tf_op jit(solution)/shard_map/gather/ppermute | solution.py:23
  143.2 8.1 %collective-permute-start.26 = (f32[4,128,256]{2,1,0:T(8,128)S(1)}, f32[4,128,256]{2,1,0:T(8,128)S(1)}, u32[]{:S(2)}, u32[]{:S(2)}) collective-permute-start(f32[4,128,256]{2,1,0:T(8,128)S(1)} %get-tuple-element.11), channel_id=1, source_target_pairs={{0,24},{8,0},{16,8},{24,16},{1,25},{9,1},{17,9},{25,17},{2,26},{10... | collective-permute-start | bytes 1572872 | tf_op jit(solution)/shard_map/scatter_rows/ppermute | solution.py:23
  145.0 9.5 %collective-permute-start.24 = (f32[4,128,256]{2,1,0:T(8,128)S(1)}, f32[4,128,256]{2,1,0:T(8,128)S(1)}, u32[]{:S(2)}, u32[]{:S(2)}) collective-permute-start(f32[4,128,256]{2,1,0:T(8,128)S(1)} %get-tuple-element.9), channel_id=1, source_target_pairs={{0,8},{8,16},{16,24},{24,0},{1,9},{9,17},{17,25},{25,1},{2,10},{10... | collective-permute-start | bytes 1572872 | tf_op jit(solution)/shard_map/scatter_rows/ppermute | solution.py:23
  151.5 21.0 %collective-permute-start.27 = (f32[8,128,256]{2,1,0:T(8,128)S(1)}, f32[8,128,256]{2,1,0:T(8,128)S(1)}, u32[]{:S(2)}, u32[]{:S(2)}) collective-permute-start(f32[8,128,256]{2,1,0:T(8,128)S(1)} %pad_maximum_fusion.1), channel_id=1, source_target_pairs={{0,24},{8,0},{16,8},{24,16},{1,25},{9,1},{17,9},{25,17},{2,26},{10... | collective-permute-start | bytes 3145736 | tf_op jit(solution)/shard_map/scatter_rows/ppermute | solution.py:23
  154.7 21.2 %collective-permute-start.25 = (f32[8,128,256]{2,1,0:T(8,128)S(1)}, f32[8,128,256]{2,1,0:T(8,128)S(1)}, u32[]{:S(2)}, u32[]{:S(2)}) collective-permute-start(f32[8,128,256]{2,1,0:T(8,128)S(1)} %pad_maximum_fusion), channel_id=1, source_target_pairs={{0,8},{8,16},{16,24},{24,0},{1,9},{9,17},{17,25},{25,1},{2,10},{10... | collective-permute-start | bytes 3145736 | tf_op jit(solution)/shard_map/scatter_rows/ppermute | solution.py:23

commit v2 on v1

v2 whole, which is shorter than its diff:
```python
import functools

import jax
import jax.numpy as jnp
from jax import lax
from jax.experimental import pallas as pl
from jax.experimental.pallas import tpu as pltpu
from jax.sharding import Mesh
from jax.sharding import PartitionSpec as P

AXES = ("y", "core", "x", "z")
SIZES = (4, 2, 4, 8)
EDGE = 128
WIDTH = 256
BLOCKS = 32
BUCKETS = 32
PER_BUCKET = 6
SLOTS = 192
ROWS = 32768
GROUP = 4


def shift(value, axis, step):
    count = lax.axis_size(axis)
    return lax.ppermute(value, axis, [(i, (i + step) % count) for i in range(count)])


def ring_gather(block, axis):
    count = lax.axis_size(axis)
    found = [None] * count
    found[0] = (block,)
    behind = ahead = block
    for step in range(1, count // 2):
        behind = shift(behind, axis, 1)
        ahead = shift(ahead, axis, -1)
        found[count - step] = (behind,)
        found[step] = (ahead,)
    half = block.shape[0] // 2
    found[count // 2] = (shift(behind[:half], axis, 1), shift(ahead[half:], axis, -1))
    return found


def join(blocks):
    return jnp.concatenate([part for block in blocks for part in block], axis=0)


def products_kernel(part, fill, blk, side, row, tiles, *refs):
    if part == 0:
        first, second, total = refs[:3]
        panels, held, order, tile_sem, piece_sem = refs[3:]
    else:
        first, second, before, total = refs[:4]
        panels, held, order, tile_sem, piece_sem, before_sem = refs[4:]
    length = first.shape[0]
    copies = [
        pltpu.make_async_copy(first, panels.at[pl.ds(0, length)], piece_sem.at[0]),
        pltpu.make_async_copy(second, panels.at[pl.ds(length, length)], piece_sem.at[1]),
    ]
    if part == 1:
        copies.append(pltpu.make_async_copy(before, total, before_sem))
    for copy in copies:
        copy.start()

    def tile_copy(i):
        return pltpu.make_async_copy(tiles.at[order[i]], held.at[i], tile_sem.at[i])

    def list_bucket(b, count):
        def put(j, c):
            slot = b * PER_BUCKET + j
            wanted = side[slot] == part

            @pl.when(wanted)
            def _():
                order[c] = slot
                tile_copy(c).start()

            return c + wanted.astype(jnp.int32)

        return lax.fori_loop(0, fill[b], put, count)

    count = lax.fori_loop(0, BUCKETS, list_bucket, 0)
    if part == 0:
        total[...] = jnp.zeros_like(total)

    def product(i):
        tile = held[i]
        panel = panels[pl.ds(pl.multiple_of(blk[order[i]] * EDGE, EDGE), EDGE), :]
        tile_hi = tile.astype(jnp.bfloat16)
        tile_lo = (tile - tile_hi.astype(jnp.float32)).astype(jnp.bfloat16)
        panel_hi = panel.astype(jnp.bfloat16)
        panel_lo = (panel - panel_hi.astype(jnp.float32)).astype(jnp.bfloat16)
        left = jnp.concatenate([tile_hi, tile_hi, tile_lo], axis=1)
        right = jnp.concatenate([panel_hi, panel_lo, panel_hi], axis=0)
        return jnp.dot(left, right, preferred_element_type=jnp.float32)

    for copy in copies:
        copy.wait()
    groups = count // GROUP

    @pl.loop(0, groups)
    def _(g):
        slots = [g * GROUP + n for n in range(GROUP)]
        for i in slots:
            tile_copy(i).wait()
        sums = [product(i) for i in slots]
        for i, value in zip(slots, sums):
            total[row[order[i]]] += value

    @pl.loop(groups * GROUP, count)
    def _(i):
        tile_copy(i).wait()
        total[row[order[i]]] += product(i)


def slot_products(part, tables, tiles, pieces, before=None):
    any_space = pl.BlockSpec(memory_space=pl.ANY)
    smem = pl.BlockSpec(memory_space=pltpu.SMEM)
    vmem = pl.BlockSpec(memory_space=pltpu.VMEM)
    arrays = [tiles, *pieces] + ([before] if part else [])
    scratch = [
        pltpu.VMEM((2 * pieces[0].shape[0], WIDTH), jnp.float32),
        pltpu.VMEM((SLOTS, EDGE, EDGE), jnp.float32),
        pltpu.SMEM((SLOTS,), jnp.int32),
        pltpu.SemaphoreType.DMA((SLOTS,)),
        pltpu.SemaphoreType.DMA((2,)),
    ]
    if part:
        scratch.append(pltpu.SemaphoreType.DMA)
    return pl.pallas_call(
        functools.partial(products_kernel, part),
        out_shape=jax.ShapeDtypeStruct((BLOCKS, EDGE, WIDTH), jnp.float32),
        in_specs=[smem] * 4 + [any_space] * len(arrays),
        out_specs=vmem,
        scratch_shapes=scratch,
        compiler_params=pltpu.CompilerParams(vmem_limit_bytes=40 * 1024 * 1024),
        cost_estimate=pl.CostEstimate(
            flops=3 * SLOTS * EDGE * EDGE * WIDTH, bytes_accessed=22 * 1024 * 1024, transcendentals=0
        ),
        name="slot_products",
    )(*tables, *arrays)


BAND = 64


def factor_kernel(gram, rows, embedding, factor, work):
    work[:, :WIDTH] = gram[...]
    work[:, WIDTH:] = rows[...].T
    lane = lax.broadcasted_iota(jnp.int32, (8, EDGE), 1)
    sub = lax.broadcasted_iota(jnp.int32, (8, EDGE), 0)
    columns = (WIDTH + EDGE) // EDGE

    def along_lanes(value, at):
        return jnp.broadcast_to(value[:, at : at + 1], (8, EDGE))

    def along_rows(value, at):
        return jnp.broadcast_to(value[at : at + 1, :], (8, EDGE))

    for band in range(WIDTH // BAND):
        top = band * BAND
        lead = top // EDGE
        strips = BAND // 8
        held = [
            [work[top + 8 * s : top + 8 * s + 8, c * EDGE : (c + 1) * EDGE] for c in range(lead, columns)]
            for s in range(strips)
        ]
        for s0 in range(strips):
            at = (top + 8 * s0) % EDGE
            cols = {s: [along_lanes(held[s][0], at + q) for q in range(8)] for s in range(s0, strips)}
            block = {(t, r): along_rows(cols[s0][r], t) for t in range(8) for r in range(t + 1)}
            lower = {}
            inverse = []
            root = []
            for q in range(8):
                inverse.append(1.0 / block[q, q])
                root.append(lax.rsqrt(block[q, q]))
                for t in range(q + 1, 8):
                    lower[t, q] = block[t, q] * inverse[q]
                for t in range(q + 1, 8):
                    for r in range(q + 1, t + 1):
                        block[t, r] = block[t, r] - lower[t, q] * block[r, q]
            lines = []
            for q in range(8):
                line = [along_rows(v, q) for v in held[s0]]
                for t in range(q):
                    line = [v - lower[q, t] * w for v, w in zip(line, lines[t])]
                lines.append(line)
            for s in range(s0 + 1, strips):
                weights = []
                for q in range(8):
                    value = cols[s][q]
                    for t in range(q):
                        value = value - lower[q, t] * weights[t]
                    weights.append(value)
                weights = [v * w for v, w in zip(weights, inverse)]
                for q in range(8):
                    held[s] = [v - weights[q] * w for v, w in zip(held[s], lines[q])]
            final = [jnp.zeros((8, EDGE), jnp.float32)] * len(held[s0])
            for q in range(8):
                final = [jnp.where(sub == q, w * root[q], v) for v, w in zip(final, lines[q])]
            for c in range(lead, columns):
                value = final[c - lead]
                if c < WIDTH // EDGE:
                    value = jnp.where(lane + c * EDGE >= sub + (top + 8 * s0), value, 0.0)
                work[top + 8 * s0 : top + 8 * s0 + 8, c * EDGE : (c + 1) * EDGE] = value
        below = top + BAND
        if below < WIDTH:
            base = below // EDGE * EDGE
            left = work[top:below, base:WIDTH]
            right = work[top:below, base:]
            update = lax.dot_general(
                left,
                right,
                (((0,), (0,)), ((), ())),
                precision=lax.Precision.HIGHEST,
                preferred_element_type=jnp.float32,
            )
            work[below:, base:] -= update[below - base :, :]
    scale = jnp.sqrt(jnp.float32(ROWS))
    for band in range(WIDTH // BAND):
        top = band * BAND
        lead = top // EDGE * EDGE
        if lead:
            factor[top : top + BAND, :lead] = jnp.zeros((BAND, lead), jnp.float32)
        factor[top : top + BAND, lead:] = work[top : top + BAND, lead:WIDTH] / scale
    embedding[...] = work[:, WIDTH:].T * scale


def factor_and_solve(gram, rows):
    vmem = pl.BlockSpec(memory_space=pltpu.VMEM)
    return pl.pallas_call(
        factor_kernel,
        out_shape=[
            jax.ShapeDtypeStruct((EDGE, WIDTH), jnp.float32),
            jax.ShapeDtypeStruct((WIDTH, WIDTH), jnp.float32),
        ],
        in_specs=[vmem, vmem],
        out_specs=[vmem, vmem],
        scratch_shapes=[pltpu.VMEM((WIDTH, WIDTH + EDGE), jnp.float32)],
        compiler_params=pltpu.CompilerParams(vmem_limit_bytes=16 * 1024 * 1024),
        name="factor_and_solve",
    )(gram, rows)


def exchange(value, axes):
    return lax.all_to_all(value, axes, 0, 0, tiled=True)


def on_device(tiles, tile_rows, tile_cols, bucket_fill, row_slot, sketch):
    here_x = lax.axis_index("x")
    here_z = lax.axis_index("z")
    here_core = lax.axis_index("core")

    slot_ids = jnp.arange(SLOTS, dtype=jnp.int32)
    bucket = slot_ids // PER_BUCKET
    cols = tile_cols[0, 0]
    far_x = (bucket // 8 - here_x) % 4
    far_z = (bucket % 8 - here_z) % 8
    blk = jnp.where(cols % 2 == 0, far_z * 4 + far_x, 32 + far_x * 8 + far_z)
    side = (cols // 2 + here_core) % 2
    block_ids = jnp.arange(BLOCKS, dtype=jnp.int32)
    target = jnp.sum(
        jnp.where(tile_rows[0, 0][:, None] == block_ids[None, :], row_slot[0][None, :], 0), axis=1
    )
    ahead = (target // 8 - here_x) % 4
    chunk = jnp.where(ahead == 3, 2, jnp.where(ahead == 2, 3, ahead))
    row = chunk * 8 + target % 8

    with jax.named_scope("gather"):
        mine = lax.dynamic_slice_in_dim(sketch, here_core * 2 * EDGE, 2 * EDGE, 0)
        slab = join(ring_gather(mine[:EDGE], "x"))
        line = join(ring_gather(mine[EDGE:], "z"))
        first = join(ring_gather(slab, "z"))
        second = join(ring_gather(line, "x"))
        first_other = shift(first, "core", 1)
        second_other = shift(second, "core", 1)

    tables = (bucket_fill[0, 0], blk, side, row)
    sums = slot_products(0, tables, tiles[0, 0], (first, second))
    sums = slot_products(1, tables, tiles[0, 0], (first_other, second_other), sums)

    with jax.named_scope("scatter_rows"):
        own, up, down, far_up, far_down = (
            sums[:8], sums[8:16], sums[16:24], sums[24:28], sums[28:32]
        )
        from_below = shift(far_up, "x", 1)
        from_above = shift(far_down, "x", -1)
        up = jnp.concatenate([up[:4] + from_below, up[4:]], axis=0)
        down = jnp.concatenate([down[:4], down[4:] + from_above], axis=0)
        own = own + shift(up, "x", 1) + shift(down, "x", -1)
        product_rows = jnp.sum(exchange(own, "z"), axis=0)

    with jax.named_scope("gram"):
        gram = jnp.dot(
            product_rows.T,
            product_rows,
            precision=lax.Precision.HIGHEST,
            preferred_element_type=jnp.float32,
        )
        ring = ("y", "core", "x")
        part = jnp.sum(exchange(gram, ring).reshape(32, 8, WIDTH), axis=0)
        part = jnp.sum(
            exchange(jnp.broadcast_to(part[None], (8, 8, WIDTH)), "z"), axis=0
        )
        gram = exchange(jnp.broadcast_to(part[None], (32, 8, WIDTH)), ring).reshape(WIDTH, WIDTH)

    embedding, factor = factor_and_solve(gram, product_rows)
    return embedding, factor


def solution(mesh):
    fine = Mesh(mesh.devices.reshape(SIZES), AXES)
    grp, col = ("y", "core"), ("x", "z")
    placed = (
        P(grp, col, None, None, None),
        P(grp, col, None),
        P(grp, col, None),
        P(grp, col, None),
        P(grp, None),
        P(col, None),
    )
    return jax.shard_map(
        on_device,
        mesh=fine,
        in_specs=placed,
        out_specs=(P(AXES, None), P()),
        check_vma=False,
    )
```

time: 287 us -> 250 us (0.87)
  waiting for transfers between devices: 108 us -> 72.7 us
  Pallas kernels: 53.9 us -> 31.8 us
  local copies, waits for them, and re-layouts: 4.62 us -> 22.1 us
    ppermute x28 -> x30, waiting for transfers between devices: 108 us -> 72.7 us  [shift(): lax.ppermute(value, axis, [(i, (i + step) % count) for i in range(count)])]
    pallas_call x1, Pallas kernels: 35.3 us -> 9.67 us  [factor_and_solve(): pl.pallas_call(factor_kernel, out_shape=[jax.ShapeDtypeStruct((EDGE, WIDT...]
    unnamed x38 -> x32, local copies, waits for them, and re-layouts: 0.21 us -> 18.6 us
    pallas_call x1 -> x2, Pallas kernels: 18.6 us -> 22.1 us  [slot_products(): pl.pallas_call(functools.partial(products_kernel, part), out_shape=jax.Sh...]
    concatenate x2 -> x4, local copies, waits for them, and re-layouts: 0.04 us -> 3.22 us  [join(): return jnp.concatenate([part for block in blocks for part in block], axis=0)]
    ppermute x28 -> x30, starting transfers between devices: 43.7 us -> 45.9 us  [shift(): lax.ppermute(value, axis, [(i, (i + step) % count) for i in range(count)])]
  transfers between devices with their start and end apart: 28 -> 30, of which waited for: 14 -> 9; matrix products, arithmetic and copies ran while one was open for 1% -> 8% of each run, Pallas kernels for 0% -> 5%
where the time goes in v2:
time: 250 us; the launch traced here: 249 us
  blocking collectives  74.8 us (30%)
  waiting for transfers between devices  72.7 us (29%)
  starting transfers between devices  45.9 us (18%)
  Pallas kernels  31.8 us (13%)
  local copies, waits for them, and re-layouts  22.1 us (9%)
    all_to_all x4, blocking collectives, exchange(): return lax.all_to_all(value, axes, 0, 0, tiled=True)  74.8 us
    ppermute x30, waiting for transfers between devices, shift(): lax.ppermute(value, axis, [(i, (i + step) % count) for i in range(count)])  72.7 us
    ppermute x30, starting transfers between devices, shift(): lax.ppermute(value, axis, [(i, (i + step) % count) for i in range(count)])  45.9 us
    pallas_call x2, Pallas kernels, slot_products(): pl.pallas_call(functools.partial(products_kernel, part), out_shape=jax.Sh...  22.1 us
    unnamed x32, local copies, waits for them, and re-layouts  18.6 us
    pallas_call x1, Pallas kernels, factor_and_solve(): pl.pallas_call(factor_kernel, out_shape=[jax.ShapeDtypeStruct((EDGE, WIDT...  9.67 us
  transfers between devices with their start and end apart: 30, of which 9 were waited for; matrix products, arithmetic and copies ran while one was open for 8% of the time, Pallas kernels for 5%

profile of v2, /device:TPU:1, one launch (start us, length us, event | category | flops | bytes accessed | tf_op | source)
XLA Modules:
  0.0 249.4 jit_solution(9310558109557619615)
XLA Ops:
  0.6 1.0 constant_dynamic-update-slice_fusion.26
  1.7 2.1 collective-permute-start.1
  3.8 1.4 collective-permute-start
  5.1 5.7 %collective-permute-start.13 = (f32[128,256]{1,0:T(8,128)S(1)}, f32[128,256]{1,0:T(8,128)S(1)}, u32[]{:S(2)}, u32[]{:S(2)}) collective-permute-start(f32[128,256]{1,0:T(8,128)S(1)} %get-tuple-element.3), channel_id=1, source_target_pairs={{0,7},{1,0},{2,1},{3,2},{4,3},{5,4},{6,5},{7,6},{8,15},{9,8},{10,9... | collective-permute-start | bytes 393224 | tf_op jit(solution)/shard_map/gather/ppermute | solution.py:25
  10.8 0.7 constant_dynamic-update-slice_fusion.17
  11.7 2.7 %collective-permute-start.3 = (f32[64,256]{1,0:T(8,128)S(1)}, f32[64,256]{1,0:T(8,128)S(1)}, u32[]{:S(2)}, u32[]{:S(2)}) collective-permute-start(f32[64,256]{1,0:T(8,128)S(1)} %slice.75), channel_id=1, source_target_pairs={{0,24},{8,0},{16,8},{24,16},{1,25},{9,1},{17,9},{25,17},{2,26},{10... | collective-permute-start | bytes 196616 | tf_op jit(solution)/shard_map/gather/ppermute | solution.py:25
  14.4 2.7 %collective-permute-start.14 = (f32[128,256]{1,0:T(8,128)S(1)}, f32[128,256]{1,0:T(8,128)S(1)}, u32[]{:S(2)}, u32[]{:S(2)}) collective-permute-start(f32[128,256]{1,0:T(8,128)S(1)} %collective-permute-done.13), channel_id=1, source_target_pairs={{0,7},{1,0},{2,1},{3,2},{4,3},{5,4},{6,5},{7,6},{8,15},{9,8},{10,9... | collective-permute-start | bytes 393224 | tf_op jit(solution)/shard_map/gather/ppermute | solution.py:25
  17.1 0.7 constant_dynamic-update-slice_fusion.25
  17.7 0.7 constant_dynamic-update-slice_fusion.3
  18.4 0.6 constant_dynamic-update-slice_fusion.2
  19.1 0.6 constant_dynamic-update-slice_fusion.1
  19.7 2.7 %collective-permute-start.15 = (f32[128,256]{1,0:T(8,128)S(1)}, f32[128,256]{1,0:T(8,128)S(1)}, u32[]{:S(2)}, u32[]{:S(2)}) collective-permute-start(f32[128,256]{1,0:T(8,128)S(1)} %collective-permute-done.14), channel_id=1, source_target_pairs={{0,7},{1,0},{2,1},{3,2},{4,3},{5,4},{6,5},{7,6},{8,15},{9,8},{10,9... | collective-permute-start | bytes 393224 | tf_op jit(solution)/shard_map/gather/ppermute | solution.py:25
  22.4 0.7 constant_dynamic-update-slice_fusion
  23.1 2.7 %collective-permute-start.4 = (f32[512,256]{1,0:T(8,128)S(1)}, f32[512,256]{1,0:T(8,128)S(1)}, u32[]{:S(2)}, u32[]{:S(2)}) collective-permute-start(f32[512,256]{1,0:T(8,128)S(1)} %get-tuple-element.24), channel_id=1, source_target_pairs={{0,7},{1,0},{2,1},{3,2},{4,3},{5,4},{6,5},{7,6},{8,15},{9,8},{10,9... | collective-permute-start | bytes 1572872 | tf_op jit(solution)/shard_map/gather/ppermute | solution.py:25
  25.7 0.7 constant_dynamic-update-slice_fusion.24
  26.4 1.0 collective-permute-done.18
  27.4 2.7 %collective-permute-start.20 = (f32[64,256]{1,0:T(8,128)S(1)}, f32[64,256]{1,0:T(8,128)S(1)}, u32[]{:S(2)}, u32[]{:S(2)}) collective-permute-start(f32[64,256]{1,0:T(8,128)S(1)} %slice.79), channel_id=1, source_target_pairs={{0,7},{1,0},{2,1},{3,2},{4,3},{5,4},{6,5},{7,6},{8,15},{9,8},{10,9... | collective-permute-start | bytes 196616 | tf_op jit(solution)/shard_map/gather/ppermute | solution.py:25
  30.2 0.7 constant_dynamic-update-slice_fusion.23
  30.8 9.7 %collective-permute-done.19 = f32[64,256]{1,0:T(8,128)S(1)} collective-permute-done((f32[64,256]{1,0:T(8,128)S(1)}, f32[64,256]{1,0:T(8,128)S(1)}, u32[]{:S(2)}, u32[]{:S(2)}) %collective-permute-start.19) | collective-permute-done | bytes 65568 | tf_op jit(solution)/shard_map/gather/ppermute | solution.py:25
  40.5 0.6 constant_dynamic-update-slice_fusion.22
  41.1 0.6 constant_dynamic-update-slice_fusion.21
  41.8 0.7 constant_dynamic-update-slice_fusion.20
  42.4 0.7 constant_dynamic-update-slice_fusion.19
  43.1 0.7 constant_dynamic-update-slice_fusion.18
  43.8 2.7 %collective-permute-start.21 = (f32[1024,256]{1,0:T(8,128)S(1)}, f32[1024,256]{1,0:T(8,128)S(1)}, u32[]{:S(2)}, u32[]{:S(2)}) collective-permute-start(f32[1024,256]{1,0:T(8,128)S(1)} %get-tuple-element.12), channel_id=1, source_target_pairs={{0,24},{8,0},{16,8},{24,16},{1,25},{9,1},{17,9},{25,17},{2,26},{10... | collective-permute-start | bytes 3145736 | tf_op jit(solution)/shard_map/gather/ppermute | solution.py:25
  46.4 2.7 %collective-permute-start.5 = (f32[512,256]{1,0:T(8,128)S(1)}, f32[512,256]{1,0:T(8,128)S(1)}, u32[]{:S(2)}, u32[]{:S(2)}) collective-permute-start(f32[512,256]{1,0:T(8,128)S(1)} %collective-permute-done.4), channel_id=1, source_target_pairs={{0,7},{1,0},{2,1},{3,2},{4,3},{5,4},{6,5},{7,6},{8,15},{9,8},{10,9... | collective-permute-start | bytes 1572872 | tf_op jit(solution)/shard_map/gather/ppermute | solution.py:25
  49.1 7.8 %collective-permute-done.8 = f32[512,256]{1,0:T(8,128)S(1)} collective-permute-done((f32[512,256]{1,0:T(8,128)S(1)}, f32[512,256]{1,0:T(8,128)S(1)}, u32[]{:S(2)}, u32[]{:S(2)}) %collective-permute-start.8) | collective-permute-done | bytes 524320 | tf_op jit(solution)/shard_map/gather/ppermute | solution.py:25
  56.9 2.7 %collective-permute-start.6 = (f32[512,256]{1,0:T(8,128)S(1)}, f32[512,256]{1,0:T(8,128)S(1)}, u32[]{:S(2)}, u32[]{:S(2)}) collective-permute-start(f32[512,256]{1,0:T(8,128)S(1)} %collective-permute-done.5), channel_id=1, source_target_pairs={{0,7},{1,0},{2,1},{3,2},{4,3},{5,4},{6,5},{7,6},{8,15},{9,8},{10,9... | collective-permute-start | bytes 1572872 | tf_op jit(solution)/shard_map/gather/ppermute | solution.py:25
  59.6 6.4 %collective-permute-done.22 = f32[1024,256]{1,0:T(8,128)S(1)} collective-permute-done((f32[1024,256]{1,0:T(8,128)S(1)}, f32[1024,256]{1,0:T(8,128)S(1)}, u32[]{:S(2)}, u32[]{:S(2)}) %collective-permute-start.22) | collective-permute-done | bytes 1048608 | tf_op jit(solution)/shard_map/gather/ppermute | solution.py:25
  66.2 2.7 %collective-permute-start.24 = (f32[512,256]{1,0:T(8,128)S(1)}, f32[512,256]{1,0:T(8,128)S(1)}, u32[]{:S(2)}, u32[]{:S(2)}) collective-permute-start(f32[512,256]{1,0:T(8,128)S(1)} %slice.81), channel_id=1, source_target_pairs={{0,24},{8,0},{16,8},{24,16},{1,25},{9,1},{17,9},{25,17},{2,26},{10... | collective-permute-start | bytes 1572872 | tf_op jit(solution)/shard_map/gather/ppermute | solution.py:25
  68.9 0.8 constant_dynamic-update-slice_fusion.12
  69.8 0.8 constant_dynamic-update-slice_fusion.11
  70.6 1.0 constant_dynamic-update-slice_fusion.30
  71.8 2.7 %collective-permute-start.11 = (f32[256,256]{1,0:T(8,128)S(1)}, f32[256,256]{1,0:T(8,128)S(1)}, u32[]{:S(2)}, u32[]{:S(2)}) collective-permute-start(f32[256,256]{1,0:T(8,128)S(1)} %slice.77), channel_id=1, source_target_pairs={{0,7},{1,0},{2,1},{3,2},{4,3},{5,4},{6,5},{7,6},{8,15},{9,8},{10,9... | collective-permute-start | bytes 786440 | tf_op jit(solution)/shard_map/gather/ppermute | solution.py:25
  74.5 0.8 constant_dynamic-update-slice_fusion.10
  75.3 1.1 collective-permute-done.23
  76.4 0.8 constant_dynamic-update-slice_fusion.29
  77.3 0.8 constant_dynamic-update-slice_fusion.28
  78.1 1.1 constant_dynamic-update-slice_fusion.27.refs_1_
  79.1 5.4 %collective-permute-start.25 = (f32[4096,256]{1,0:T(8,128)}, f32[4096,256]{1,0:T(8,128)}, u32[]{:S(2)}, u32[]{:S(2)}) collective-permute-start(f32[4096,256]{1,0:T(8,128)} %constant_dynamic-update-slice_fusion.27.refs_1_), channel_id=1, source_target_pairs={{0,32},{32,0},{1,33},{33,1},{2,34},{34,2},{3,35},{35,3},{4,36},{36... | collective-permute-start | bytes 12582920 | tf_op jit(solution)/shard_map/gather/ppermute | solution.py:25
  84.5 0.7 constant_dynamic-update-slice_fusion.9
  85.2 0.7 constant_dynamic-update-slice_fusion.8
  86.0 0.8 constant_dynamic-update-slice_fusion.7
  86.8 0.8 constant_dynamic-update-slice_fusion.6
  87.6 0.8 constant_dynamic-update-slice_fusion.5.refs_0_
  88.5 0.1 select_reduce_fusion
  88.6 11.4 %slot_products.2.refs_2_ = f32[32,128,256]{2,1,0:T(8,128)S(1)} custom-call(s32[32]{0:T(128)S(1)} %bitcast.15, s32[192]{0:T(256)S(1)} %get-tuple-element.37.blk, s32[192]{0:T(256)S(1)} %get-tuple-element.36.side, s32[192]{0:T(256)S(1)} %fusion.6.row, f32[192,128,128]{2,1,0:T(8,128)} %bitcast.17, f32[4096,256]{1,0:T(8,128)} %constant_dynamic-update-slice_fusion.5.refs_0_, ...), custom_call_target="tpu_custom_call" | custom-call | flops 2415919104 | bytes 23068672 | tf_op jit(solution)/shard_map/slot_products/pallas_call | solution.py:129
  100.1 2.0 copy-done
  102.1 10.7 %slot_products.3 = f32[32,128,256]{2,1,0:T(8,128)S(1)} custom-call(s32[32]{0:T(128)S(1)} %bitcast.16, s32[192]{0:T(256)S(1)} %get-tuple-element.37.blk, s32[192]{0:T(256)S(1)} %get-tuple-element.36.side, s32[192]{0:T(256)S(1)} %fusion.6.row, f32[192,128,128]{2,1,0:T(8,128)} %bitcast.18, f32[4096,256]{1,0:T(8,128)} %collective-permute-done.12.refs_0_, ...), custom_call_target="tpu_custom_call" | custom-call | flops 2415919104 | bytes 23068672 | tf_op jit(solution)/shard_map/slot_products/pallas_call | solution.py:129
  112.9 14.9 %collective-permute-done.26 = f32[4,128,256]{2,1,0:T(8,128)S(1)} collective-permute-done((f32[4,128,256]{2,1,0:T(8,128)S(1)}, f32[4,128,256]{2,1,0:T(8,128)S(1)}, u32[]{:S(2)}, u32[]{:S(2)}) %collective-permute-start.26) | collective-permute-done | bytes 524320 | tf_op jit(solution)/shard_map/scatter_rows/ppermute | solution.py:25
  127.8 0.2 slice_add_fusion.2
  128.0 1.3 collective-permute-start.28
  129.4 0.5 collective-permute-start.27
  129.9 10.9 %collective-permute-done.28 = f32[4,128,256]{2,1,0:T(8,128)S(1)} collective-permute-done((f32[4,128,256]{2,1,0:T(8,128)S(1)}, f32[4,128,256]{2,1,0:T(8,128)S(1)}, u32[]{:S(2)}, u32[]{:S(2)}) %collective-permute-start.28) | collective-permute-done | bytes 524320 | tf_op jit(solution)/shard_map/scatter_rows/ppermute | solution.py:25
  141.0 2.2 collective-permute-start.29
  143.2 11.1 %collective-permute-done.27 = f32[8,128,256]{2,1,0:T(8,128)S(1)} collective-permute-done((f32[8,128,256]{2,1,0:T(8,128)S(1)}, f32[8,128,256]{2,1,0:T(8,128)S(1)}, u32[]{:S(2)}, u32[]{:S(2)}) %collective-permute-start.27) | collective-permute-done | bytes 1048608 | tf_op jit(solution)/shard_map/scatter_rows/ppermute | solution.py:25
  154.3 9.8 %collective-permute-done.29 = f32[8,128,256]{2,1,0:T(8,128)S(1)} collective-permute-done((f32[8,128,256]{2,1,0:T(8,128)S(1)}, f32[8,128,256]{2,1,0:T(8,128)S(1)}, u32[]{:S(2)}, u32[]{:S(2)}) %collective-permute-start.29) | collective-permute-done | bytes 1048608 | tf_op jit(solution)/shard_map/scatter_rows/ppermute | solution.py:25
  164.1 0.2 fusion
  164.3 33.4 %all_to_all.21 = f32[8,128,256]{2,1,0:T(8,128)S(1)} all-to-all(f32[8,128,256]{2,1,0:T(8,128)S(1)} %fusion), channel_id=1, replica_groups=mesh['y'=4,'core'=2,'x'=4,'z'=8] {'z'}, dimensions={0} | all-to-all | bytes 2097152 | tf_op jit(solution)/shard_map/scatter_rows/all_to_all | solution.py:246
  197.9 0.4 fusion.1
  198.3 17.8 %all_to_all.22 = f32[32,8,256]{2,1,0:T(8,128)S(1)} all-to-all(f32[32,8,256]{2,1,0:T(8,128)S(1)} %fusion.1), channel_id=1, replica_groups=mesh['y'=4,'core'=2,'x'=4,'z'=8] {'y','core','x'}, dimensions={0} | all-to-all | bytes 524288 | tf_op jit(solution)/shard_map/gram/all_to_all | solution.py:246
  216.1 9.5 %all_to_all.23 = f32[8,8,256]{2,1,0:T(8,128)S(1)} all-to-all(f32[8,8,256]{2,1,0:T(8,128)S(1)} %broadcast_in_dim.33), channel_id=1, replica_groups=mesh['y'=4,'core'=2,'x'=4,'z'=8] {'z'}, dimensions={0} | all-to-all | bytes 131072 | tf_op jit(solution)/shard_map/gram/all_to_all | solution.py:246
  225.6 14.0 %all_to_all.24 = f32[32,8,256]{2,1,0:T(8,128)S(1)} all-to-all(f32[32,8,256]{2,1,0:T(8,128)S(1)} %broadcast_in_dim.34), channel_id=1, replica_groups=mesh['y'=4,'core'=2,'x'=4,'z'=8] {'y','core','x'}, dimensions={0} | all-to-all | bytes 524288 | tf_op jit(solution)/shard_map/gram/all_to_all | solution.py:246
  239.7 9.7 %factor_and_solve.1 = (f32[128,256]{1,0:T(8,128)}, f32[256,256]{1,0:T(8,128)}) custom-call(f32[256,256]{1,0:T(8,128)S(1)} %bitcast.14, f32[128,256]{1,0:T(8,128)S(1)} %reduce_sum.37.rows), custom_call_target="tpu_custom_call" | custom-call | tf_op jit(solution)/shard_map/factor_and_solve/pallas_call | solution.py:231
  (63 shorter events, 1.1 us)
Async XLA Ops:
  1.7 9.9 %collective-permute-start.1 = (f32[128,256]{1,0:T(8,128)S(1)}, f32[128,256]{1,0:T(8,128)S(1)}, u32[]{:S(2)}, u32[]{:S(2)}) collective-permute-start(f32[128,256]{1,0:T(8,128)S(1)} %get-tuple-element.11), channel_id=1, source_target_pairs={{0,8},{8,16},{16,24},{24,0},{1,9},{9,17},{17,25},{25,1},{2,10},{10... | collective-permute-start | bytes 393224 | tf_op jit(solution)/shard_map/gather/ppermute | solution.py:25
  3.8 7.9 %collective-permute-start = (f32[128,256]{1,0:T(8,128)S(1)}, f32[128,256]{1,0:T(8,128)S(1)}, u32[]{:S(2)}, u32[]{:S(2)}) collective-permute-start(f32[128,256]{1,0:T(8,128)S(1)} %get-tuple-element.11), channel_id=1, source_target_pairs={{0,24},{8,0},{16,8},{24,16},{1,25},{9,1},{17,9},{25,17},{2,26},{10... | collective-permute-start | bytes 393224 | tf_op jit(solution)/shard_map/gather/ppermute | solution.py:25
  5.1 9.3 %collective-permute-start.13 = (f32[128,256]{1,0:T(8,128)S(1)}, f32[128,256]{1,0:T(8,128)S(1)}, u32[]{:S(2)}, u32[]{:S(2)}) collective-permute-start(f32[128,256]{1,0:T(8,128)S(1)} %get-tuple-element.3), channel_id=1, source_target_pairs={{0,7},{1,0},{2,1},{3,2},{4,3},{5,4},{6,5},{7,6},{8,15},{9,8},{10,9... | collective-permute-start | bytes 393224 | tf_op jit(solution)/shard_map/gather/ppermute | solution.py:25
  10.8 6.3 %collective-permute-start.16 = (f32[128,256]{1,0:T(8,128)S(1)}, f32[128,256]{1,0:T(8,128)S(1)}, u32[]{:S(2)}, u32[]{:S(2)}) collective-permute-start(f32[128,256]{1,0:T(8,128)S(1)} %get-tuple-element.3), channel_id=1, source_target_pairs={{0,1},{1,2},{2,3},{3,4},{4,5},{5,6},{6,7},{7,0},{8,9},{9,10},{10,1... | collective-permute-start | bytes 393224 | tf_op jit(solution)/shard_map/gather/ppermute | solution.py:25
  11.6 6.9 %collective-permute-start.2 = (f32[64,256]{1,0:T(8,128)S(1)}, f32[64,256]{1,0:T(8,128)S(1)}, u32[]{:S(2)}, u32[]{:S(2)}) collective-permute-start(f32[64,256]{1,0:T(8,128)S(1)} %slice.74), channel_id=1, source_target_pairs={{0,8},{8,16},{16,24},{24,0},{1,9},{9,17},{17,25},{25,1},{2,10},{10... | collective-permute-start | bytes 196616 | tf_op jit(solution)/shard_map/gather/ppermute | solution.py:25
  11.7 7.4 %collective-permute-start.3 = (f32[64,256]{1,0:T(8,128)S(1)}, f32[64,256]{1,0:T(8,128)S(1)}, u32[]{:S(2)}, u32[]{:S(2)}) collective-permute-start(f32[64,256]{1,0:T(8,128)S(1)} %slice.75), channel_id=1, source_target_pairs={{0,24},{8,0},{16,8},{24,16},{1,25},{9,1},{17,9},{25,17},{2,26},{10... | collective-permute-start | bytes 196616 | tf_op jit(solution)/shard_map/gather/ppermute | solution.py:25
  14.4 5.3 %collective-permute-start.14 = (f32[128,256]{1,0:T(8,128)S(1)}, f32[128,256]{1,0:T(8,128)S(1)}, u32[]{:S(2)}, u32[]{:S(2)}) collective-permute-start(f32[128,256]{1,0:T(8,128)S(1)} %collective-permute-done.13), channel_id=1, source_target_pairs={{0,7},{1,0},{2,1},{3,2},{4,3},{5,4},{6,5},{7,6},{8,15},{9,8},{10,9... | collective-permute-start | bytes 393224 | tf_op jit(solution)/shard_map/gather/ppermute | solution.py:25
  17.1 5.3 %collective-permute-start.17 = (f32[128,256]{1,0:T(8,128)S(1)}, f32[128,256]{1,0:T(8,128)S(1)}, u32[]{:S(2)}, u32[]{:S(2)}) collective-permute-start(f32[128,256]{1,0:T(8,128)S(1)} %collective-permute-done.16), channel_id=1, source_target_pairs={{0,1},{1,2},{2,3},{3,4},{4,5},{5,6},{6,7},{7,0},{8,9},{9,10},{10,1... | collective-permute-start | bytes 393224 | tf_op jit(solution)/shard_map/gather/ppermute | solution.py:25
  19.7 7.7 %collective-permute-start.15 = (f32[128,256]{1,0:T(8,128)S(1)}, f32[128,256]{1,0:T(8,128)S(1)}, u32[]{:S(2)}, u32[]{:S(2)}) collective-permute-start(f32[128,256]{1,0:T(8,128)S(1)} %collective-permute-done.14), channel_id=1, source_target_pairs={{0,7},{1,0},{2,1},{3,2},{4,3},{5,4},{6,5},{7,6},{8,15},{9,8},{10,9... | collective-permute-start | bytes 393224 | tf_op jit(solution)/shard_map/gather/ppermute | solution.py:25
  22.4 5.0 %collective-permute-start.18 = (f32[128,256]{1,0:T(8,128)S(1)}, f32[128,256]{1,0:T(8,128)S(1)}, u32[]{:S(2)}, u32[]{:S(2)}) collective-permute-start(f32[128,256]{1,0:T(8,128)S(1)} %collective-permute-done.17), channel_id=1, source_target_pairs={{0,1},{1,2},{2,3},{3,4},{4,5},{5,6},{6,7},{7,0},{8,9},{9,10},{10,1... | collective-permute-start | bytes 393224 | tf_op jit(solution)/shard_map/gather/ppermute | solution.py:25
  23.1 23.4 %collective-permute-start.4 = (f32[512,256]{1,0:T(8,128)S(1)}, f32[512,256]{1,0:T(8,128)S(1)}, u32[]{:S(2)}, u32[]{:S(2)}) collective-permute-start(f32[512,256]{1,0:T(8,128)S(1)} %get-tuple-element.24), channel_id=1, source_target_pairs={{0,7},{1,0},{2,1},{3,2},{4,3},{5,4},{6,5},{7,6},{8,15},{9,8},{10,9... | collective-permute-start | bytes 1572872 | tf_op jit(solution)/shard_map/gather/ppermute | solution.py:25
  25.7 20.7 %collective-permute-start.7 = (f32[512,256]{1,0:T(8,128)S(1)}, f32[512,256]{1,0:T(8,128)S(1)}, u32[]{:S(2)}, u32[]{:S(2)}) collective-permute-start(f32[512,256]{1,0:T(8,128)S(1)} %get-tuple-element.24), channel_id=1, source_target_pairs={{0,1},{1,2},{2,3},{3,4},{4,5},{5,6},{6,7},{7,0},{8,9},{9,10},{10,1... | collective-permute-start | bytes 1572872 | tf_op jit(solution)/shard_map/gather/ppermute | solution.py:25
  27.4 13.1 %collective-permute-start.19 = (f32[64,256]{1,0:T(8,128)S(1)}, f32[64,256]{1,0:T(8,128)S(1)}, u32[]{:S(2)}, u32[]{:S(2)}) collective-permute-start(f32[64,256]{1,0:T(8,128)S(1)} %slice.78), channel_id=1, source_target_pairs={{0,1},{1,2},{2,3},{3,4},{4,5},{5,6},{6,7},{7,0},{8,9},{9,10},{10,1... | collective-permute-start | bytes 196616 | tf_op jit(solution)/shard_map/gather/ppermute | solution.py:25
  27.4 13.7 %collective-permute-start.20 = (f32[64,256]{1,0:T(8,128)S(1)}, f32[64,256]{1,0:T(8,128)S(1)}, u32[]{:S(2)}, u32[]{:S(2)}) collective-permute-start(f32[64,256]{1,0:T(8,128)S(1)} %slice.79), channel_id=1, source_target_pairs={{0,7},{1,0},{2,1},{3,2},{4,3},{5,4},{6,5},{7,6},{8,15},{9,8},{10,9... | collective-permute-start | bytes 196616 | tf_op jit(solution)/shard_map/gather/ppermute | solution.py:25
  43.8 22.3 %collective-permute-start.22 = (f32[1024,256]{1,0:T(8,128)S(1)}, f32[1024,256]{1,0:T(8,128)S(1)}, u32[]{:S(2)}, u32[]{:S(2)}) collective-permute-start(f32[1024,256]{1,0:T(8,128)S(1)} %get-tuple-element.12), channel_id=1, source_target_pairs={{0,8},{8,16},{16,24},{24,0},{1,9},{9,17},{17,25},{25,1},{2,10},{10... | collective-permute-start | bytes 3145736 | tf_op jit(solution)/shard_map/gather/ppermute | solution.py:25
  43.8 22.4 %collective-permute-start.21 = (f32[1024,256]{1,0:T(8,128)S(1)}, f32[1024,256]{1,0:T(8,128)S(1)}, u32[]{:S(2)}, u32[]{:S(2)}) collective-permute-start(f32[1024,256]{1,0:T(8,128)S(1)} %get-tuple-element.12), channel_id=1, source_target_pairs={{0,24},{8,0},{16,8},{24,16},{1,25},{9,1},{17,9},{25,17},{2,26},{10... | collective-permute-start | bytes 3145736 | tf_op jit(solution)/shard_map/gather/ppermute | solution.py:25
  46.4 10.5 %collective-permute-start.8 = (f32[512,256]{1,0:T(8,128)S(1)}, f32[512,256]{1,0:T(8,128)S(1)}, u32[]{:S(2)}, u32[]{:S(2)}) collective-permute-start(f32[512,256]{1,0:T(8,128)S(1)} %collective-permute-done.7), channel_id=1, source_target_pairs={{0,1},{1,2},{2,3},{3,4},{4,5},{5,6},{6,7},{7,0},{8,9},{9,10},{10,1... | collective-permute-start | bytes 1572872 | tf_op jit(solution)/shard_map/gather/ppermute | solution.py:25
  46.4 10.5 %collective-permute-start.5 = (f32[512,256]{1,0:T(8,128)S(1)}, f32[512,256]{1,0:T(8,128)S(1)}, u32[]{:S(2)}, u32[]{:S(2)}) collective-permute-start(f32[512,256]{1,0:T(8,128)S(1)} %collective-permute-done.4), channel_id=1, source_target_pairs={{0,7},{1,0},{2,1},{3,2},{4,3},{5,4},{6,5},{7,6},{8,15},{9,8},{10,9... | collective-permute-start | bytes 1572872 | tf_op jit(solution)/shard_map/gather/ppermute | solution.py:25
  56.9 14.7 %collective-permute-start.9 = (f32[512,256]{1,0:T(8,128)S(1)}, f32[512,256]{1,0:T(8,128)S(1)}, u32[]{:S(2)}, u32[]{:S(2)}) collective-permute-start(f32[512,256]{1,0:T(8,128)S(1)} %collective-permute-done.8), channel_id=1, source_target_pairs={{0,1},{1,2},{2,3},{3,4},{4,5},{5,6},{6,7},{7,0},{8,9},{9,10},{10,1... | collective-permute-start | bytes 1572872 | tf_op jit(solution)/shard_map/gather/ppermute | solution.py:25
  56.9 14.8 %collective-permute-start.6 = (f32[512,256]{1,0:T(8,128)S(1)}, f32[512,256]{1,0:T(8,128)S(1)}, u32[]{:S(2)}, u32[]{:S(2)}) collective-permute-start(f32[512,256]{1,0:T(8,128)S(1)} %collective-permute-done.5), channel_id=1, source_target_pairs={{0,7},{1,0},{2,1},{3,2},{4,3},{5,4},{6,5},{7,6},{8,15},{9,8},{10,9... | collective-permute-start | bytes 1572872 | tf_op jit(solution)/shard_map/gather/ppermute | solution.py:25
  66.1 10.3 %collective-permute-start.23 = (f32[512,256]{1,0:T(8,128)S(1)}, f32[512,256]{1,0:T(8,128)S(1)}, u32[]{:S(2)}, u32[]{:S(2)}) collective-permute-start(f32[512,256]{1,0:T(8,128)S(1)} %slice.80), channel_id=1, source_target_pairs={{0,8},{8,16},{16,24},{24,0},{1,9},{9,17},{17,25},{25,1},{2,10},{10... | collective-permute-start | bytes 1572872 | tf_op jit(solution)/shard_map/gather/ppermute | solution.py:25
  66.2 11.0 %collective-permute-start.24 = (f32[512,256]{1,0:T(8,128)S(1)}, f32[512,256]{1,0:T(8,128)S(1)}, u32[]{:S(2)}, u32[]{:S(2)}) collective-permute-start(f32[512,256]{1,0:T(8,128)S(1)} %slice.81), channel_id=1, source_target_pairs={{0,24},{8,0},{16,8},{24,16},{1,25},{9,1},{17,9},{25,17},{2,26},{10... | collective-permute-start | bytes 1572872 | tf_op jit(solution)/shard_map/gather/ppermute | solution.py:25
  71.6 12.9 %collective-permute-start.10 = (f32[256,256]{1,0:T(8,128)S(1)}, f32[256,256]{1,0:T(8,128)S(1)}, u32[]{:S(2)}, u32[]{:S(2)}) collective-permute-start(f32[256,256]{1,0:T(8,128)S(1)} %slice.76), channel_id=1, source_target_pairs={{0,1},{1,2},{2,3},{3,4},{4,5},{5,6},{6,7},{7,0},{8,9},{9,10},{10,1... | collective-permute-start | bytes 786440 | tf_op jit(solution)/shard_map/gather/ppermute | solution.py:25
  71.8 13.5 %collective-permute-start.11 = (f32[256,256]{1,0:T(8,128)S(1)}, f32[256,256]{1,0:T(8,128)S(1)}, u32[]{:S(2)}, u32[]{:S(2)}) collective-permute-start(f32[256,256]{1,0:T(8,128)S(1)} %slice.77), channel_id=1, source_target_pairs={{0,7},{1,0},{2,1},{3,2},{4,3},{5,4},{6,5},{7,6},{8,15},{9,8},{10,9... | collective-permute-start | bytes 786440 | tf_op jit(solution)/shard_map/gather/ppermute | solution.py:25
  75.3 13.1 %copy-start.2 = (s32[1,1,192]{2,1,0:T(1,128)S(1)}, s32[1,1,192]{2,1,0:T(1,128)}, u32[]{:S(2)}) copy-start(s32[1,1,192]{2,1,0:T(1,128)} %param.7) | copy-start | bytes 2308
  75.3 13.1 %copy-start.4 = (s32[1,32]{1,0:T(1,128)S(1)}, s32[1,32]{1,0:T(1,128)}, u32[]{:S(2)}) copy-start(s32[1,32]{1,0:T(1,128)} %param.10) | copy-start | bytes 388
  75.3 13.2 %copy-start.3 = (s32[1,1,192]{2,1,0:T(1,128)S(1)}, s32[1,1,192]{2,1,0:T(1,128)}, u32[]{:S(2)}) copy-start(s32[1,1,192]{2,1,0:T(1,128)} %param.8) | copy-start | bytes 2308
  75.3 13.3 %copy-start.1 = (s32[1,1,32]{2,1,0:T(1,128)S(1)}, s32[1,1,32]{2,1,0:T(1,128)}, u32[]{:S(2)}) copy-start(s32[1,1,32]{2,1,0:T(1,128)} %param.9) | copy-start | bytes 388
  79.1 23.0 %collective-permute-start.25 = (f32[4096,256]{1,0:T(8,128)}, f32[4096,256]{1,0:T(8,128)}, u32[]{:S(2)}, u32[]{:S(2)}) collective-permute-start(f32[4096,256]{1,0:T(8,128)} %constant_dynamic-update-slice_fusion.27.refs_1_), channel_id=1, source_target_pairs={{0,32},{32,0},{1,33},{33,1},{2,34},{34,2},{3,35},{35,3},{4,36},{36... | collective-permute-start | bytes 12582920 | tf_op jit(solution)/shard_map/gather/ppermute | solution.py:25
  88.5 13.6 %collective-permute-start.12 = (f32[4096,256]{1,0:T(8,128)}, f32[4096,256]{1,0:T(8,128)}, u32[]{:S(2)}, u32[]{:S(2)}) collective-permute-start(f32[4096,256]{1,0:T(8,128)} %constant_dynamic-update-slice_fusion.5.refs_0_), channel_id=1, source_target_pairs={{0,32},{32,0},{1,33},{33,1},{2,34},{34,2},{3,35},{35,3},{4,36},{36... | collective-permute-start | bytes 12582920 | tf_op jit(solution)/shard_map/gather/ppermute | solution.py:25
  100.1 2.0 copy-start
  112.8 15.0 %collective-permute-start.26 = (f32[4,128,256]{2,1,0:T(8,128)S(1)}, f32[4,128,256]{2,1,0:T(8,128)S(1)}, u32[]{:S(2)}, u32[]{:S(2)}) collective-permute-start(f32[4,128,256]{2,1,0:T(8,128)S(1)} %slice.84), channel_id=1, source_target_pairs={{0,8},{8,16},{16,24},{24,0},{1,9},{9,17},{17,25},{25,1},{2,10},{10... | collective-permute-start | bytes 1572872 | tf_op jit(solution)/shard_map/scatter_rows/ppermute | solution.py:25
  128.0 12.8 %collective-permute-start.28 = (f32[4,128,256]{2,1,0:T(8,128)S(1)}, f32[4,128,256]{2,1,0:T(8,128)S(1)}, u32[]{:S(2)}, u32[]{:S(2)}) collective-permute-start(f32[4,128,256]{2,1,0:T(8,128)S(1)} %get-tuple-element.7), channel_id=1, source_target_pairs={{0,24},{8,0},{16,8},{24,16},{1,25},{9,1},{17,9},{25,17},{2,26},{10... | collective-permute-start | bytes 1572872 | tf_op jit(solution)/shard_map/scatter_rows/ppermute | solution.py:25
  129.4 24.9 %collective-permute-start.27 = (f32[8,128,256]{2,1,0:T(8,128)S(1)}, f32[8,128,256]{2,1,0:T(8,128)S(1)}, u32[]{:S(2)}, u32[]{:S(2)}) collective-permute-start(f32[8,128,256]{2,1,0:T(8,128)S(1)} %pad_maximum_fusion), channel_id=1, source_target_pairs={{0,8},{8,16},{16,24},{24,0},{1,9},{9,17},{17,25},{25,1},{2,10},{10... | collective-permute-start | bytes 3145736 | tf_op jit(solution)/shard_map/scatter_rows/ppermute | solution.py:25
  141.0 23.1 %collective-permute-start.29 = (f32[8,128,256]{2,1,0:T(8,128)S(1)}, f32[8,128,256]{2,1,0:T(8,128)S(1)}, u32[]{:S(2)}, u32[]{:S(2)}) collective-permute-start(f32[8,128,256]{2,1,0:T(8,128)S(1)} %pad_maximum_fusion.1), channel_id=1, source_target_pairs={{0,24},{8,0},{16,8},{24,16},{1,25},{9,1},{17,9},{25,17},{2,26},{10... | collective-permute-start | bytes 3145736 | tf_op jit(solution)/shard_map/scatter_rows/ppermute | solution.py:25
